TPU v7x, 256 devices: a whole 4x4x8 slice. The times are simulated.
256 devices in a mesh: dp: 8 (over y, x_lo), mp: 32 (over x_hi, z, core).
Axes of the slice: x: 4 (x_hi: 2, x_lo: 2; x = x_hi * 2 + x_lo), y: 4, z: 8, core: 2. Of those that a mesh axis runs over, the one named last changes fastest.
Arguments:
- activations: bfloat16 [512, 28672], P('dp', 'mp'), may hold values from -6 to 6
- out_grads: bfloat16 [512, 8192], P('mp', 'dp'), may hold values from -6 to 6
- act_basis: bfloat16 [28672, 28672], P('dp', 'mp'), may hold values from -0.03125 to 0.03125
- grad_basis: bfloat16 [8192, 8192], P('mp', 'dp'), may hold values from -0.0625 to 0.0625
Outputs:
- correction: float32 [8192, 28672], P('mp', 'dp')
All inputs are finite; a program needn't handle non-finite values.
Results may differ from a plain program's by a relative error of at most 0.0041.
Values may be sent and summed in bfloat16 or wider, within the bound.
No kernel may reach another device: no remote copies, remote signals or barrier semaphores. Data moves between devices by JAX's collectives and lax.ppermute only.
A program may use at most 64 MiB of HBM per device.

v0:
```python
import functools

import jax
import jax.numpy as jnp
from jax import lax
from jax.experimental import pallas as pl
from jax.experimental.pallas import tpu as pltpu
from jax.sharding import PartitionSpec as P

SEQ_LEN = 256
BF, F32 = jnp.bfloat16, jnp.float32
TILE = 256
STREAMS = 2


def mp_at(h, z, c):
    return ((h % 2) * 8 + z % 8) * 2 + c % 2


def dp_at(y, l):
    return (y % 4) * 2 + l % 2


def mp_perm(f):
    return [(mp_at(h, z, c), mp_at(*f(h, z, c))) for h in range(2) for z in range(8) for c in range(2)]


def dp_perm(f):
    return [(dp_at(y, l), dp_at(*f(y, l))) for y in range(4) for l in range(2)]


CORE = mp_perm(lambda h, z, c: (h, z, c + 1))
XHI = mp_perm(lambda h, z, c: (h + 1, z, c))
AHEAD = mp_perm(lambda h, z, c: (h, z + 1 - 2 * c, c))
AHEAD2 = mp_perm(lambda h, z, c: (h, z + 2 - 4 * c, c))
XLO = dp_perm(lambda y, l: (y, l + 1))
Y1 = dp_perm(lambda y, l: (y ^ 1, l))
Y2 = dp_perm(lambda y, l: (y ^ 2, l))


def swap(x, name="swap"):
    with jax.named_scope(name):
        return lax.ppermute(x, "mp", CORE)


def ahead(x, name="ahead"):
    with jax.named_scope(name):
        return lax.ppermute(x, "mp", AHEAD)


def ahead2(x, name="ahead2"):
    with jax.named_scope(name):
        return lax.ppermute(x, "mp", AHEAD2)


def across(x, name="across"):
    with jax.named_scope(name):
        return lax.ppermute(x, "mp", XHI)


def after(x, *others):
    return lax.optimization_barrier((x,) + others)[0]


def dot_t(a, b):
    return lax.dot_general(a, b, (((1,), (1,)), ((), ())), preferred_element_type=F32)


def cat(*parts):
    return jnp.concatenate(parts)


def block(step):
    return [(step, 0), (step, 1)]


def mirrored(halves):
    return [(-step if abs(step) < 4 else step, 1 - other) for step, other in halves]


LAYOUT = [[(0, 0)], [(0, 1)], block(-1), block(-2), block(-3), [(4, 0)]]
LAYOUT = LAYOUT + [mirrored(block(-1) + block(-2)), mirrored(block(-3) + [(4, 0)])]


def finish_kernel(width, first, aliased, place_ref, g_ref, *refs):
    blocks, refs = refs[: len(LAYOUT)], refs[len(LAYOUT) + aliased :]
    out_ref, act, tile, out_sem = refs
    z, c, y, l = [place_ref[i] for i in range(4)]
    for ref, halves in zip(blocks, LAYOUT):
        for i, (step, other) in enumerate(halves):
            b = lax.rem(z + (1 - 2 * c) * step + 16, 8)
            source = lax.rem(y + 4 - b // 2, 4) * 2 + lax.rem(l + b, 2)
            row = pl.multiple_of(source * 64 + (1 - c if other else c) * 32, 32)
            act[pl.ds(row, 32)] = ref[i * 32 : (i + 1) * 32]
    writes = []
    for t in range(width // TILE):
        total = None
        for s in range(2):
            rows = slice(s * SEQ_LEN, (s + 1) * SEQ_LEN)
            part = jnp.dot(g_ref[:, rows], act[rows, t * TILE : (t + 1) * TILE], preferred_element_type=F32)
            total = part * part if total is None else total + part * part
        tile[t] = total * F32(1 / 512)
        write = pltpu.make_async_copy(tile.at[t], out_ref.at[:, pl.ds(first + t * TILE, TILE)], out_sem.at[t])
        write.start()
        writes.append(write)
    for write in writes:
        write.wait()


def finish(place, g, blocks, width, first, whole, rest):
    aliased = rest is not None
    vmem, hbm = pl.BlockSpec(memory_space=pltpu.VMEM), pl.BlockSpec(memory_space=pl.ANY)
    tiles = width // TILE
    return pl.pallas_call(
        functools.partial(finish_kernel, width, first, int(aliased)),
        out_shape=jax.ShapeDtypeStruct((256, whole), F32),
        in_specs=[pl.BlockSpec(memory_space=pltpu.SMEM)] + [vmem] * (1 + len(blocks)) + [hbm] * aliased,
        out_specs=hbm,
        scratch_shapes=[
            pltpu.VMEM((512, width), BF),
            pltpu.VMEM((tiles, 256, TILE), F32),
            pltpu.SemaphoreType.DMA((tiles,)),
        ],
        input_output_aliases={2 + len(blocks): 0} if aliased else {},
        compiler_params=pltpu.CompilerParams(vmem_limit_bytes=12 * 1024 * 1024),
        cost_estimate=pl.CostEstimate(flops=2 * 512 * 256 * width, bytes_accessed=width * (1024 + 1024), transcendentals=0),
        name="finish",
    )(place, g, *blocks, *([rest] if aliased else []))


def quarters(halves):
    return [(step, other, pair) for step, other in halves for pair in (0, 1)]


N0 = quarters(block(0))
NEAR = quarters(block(-2) + block(-1) + block(-3) + [(4, 0)])
FAR = quarters(mirrored(block(-2) + block(-1) + block(-3) + [(4, 0)]))


def rotate_grads_kernel(place_ref, n0_ref, near_ref, far_ref, basis_ref, out_ref, rows):
    z, c, h = place_ref[0], place_ref[1], place_ref[4]
    for ref, pieces in ((n0_ref, N0), (near_ref, NEAR), (far_ref, FAR)):
        for piece, (step, other, pair) in enumerate(pieces):
            z2 = lax.rem(z + (1 - 2 * c) * step + 16, 8)
            h2 = 1 - h if pair else h
            c2 = 1 - c if other else c
            row = pl.multiple_of(((h2 * 8 + z2) * 2 + c2) * 16, 16)
            rows[pl.ds(row, 16)] = ref[piece * 16 : (piece + 1) * 16]
    out_ref[...] = lax.dot_general(
        basis_ref[...], rows[...], (((1,), (1,)), ((), ())), preferred_element_type=F32
    )


def rotate_grads(place, n0, near, far, basis):
    vmem = pl.BlockSpec(memory_space=pltpu.VMEM)
    return pl.pallas_call(
        rotate_grads_kernel,
        out_shape=jax.ShapeDtypeStruct((256, 512), F32),
        in_specs=[pl.BlockSpec(memory_space=pltpu.SMEM)] + [vmem] * 4,
        out_specs=vmem,
        scratch_shapes=[pltpu.VMEM((512, 1024), BF)],
        compiler_params=pltpu.CompilerParams(vmem_limit_bytes=8 * 1024 * 1024),
        cost_estimate=pl.CostEstimate(flops=2 * 512 * 256 * 1024, bytes_accessed=2 << 20, transcendentals=0),
        name="rotate_grads",
    )(place, n0, near, far, basis)


def arrange_kernel(place_ref, *refs):
    blocks, (mine_ref, theirs_ref, rows) = refs[:8], refs[8:]
    z, c = place_ref[0], place_ref[1]
    for b, ref in enumerate(blocks):
        k = lax.rem((b - z) * (1 - 2 * c) + 16, 8)
        for core in range(2):
            other = jnp.where(c == core, 0, 1)
            centre = jnp.where(k == 0, 224, 192) + other * 256
            ring = jnp.where(k < 4, (k - 1) * 64 + other * 32, 256 + (7 - k) * 64 + (1 - other) * 32)
            row = pl.multiple_of(jnp.where((k == 0) | (k == 4), centre, ring), 32)
            rows[pl.ds(row, 32)] = ref[core * 32 : core * 32 + 32]
    mine_ref[...] = rows[:256]
    theirs_ref[...] = rows[256:]


def arrange(place, blocks):
    vmem = pl.BlockSpec(memory_space=pltpu.VMEM)
    depth = blocks[0].shape[1]
    rows = jax.ShapeDtypeStruct((256, depth), BF)
    return pl.pallas_call(
        arrange_kernel,
        out_shape=(rows, rows),
        in_specs=[pl.BlockSpec(memory_space=pltpu.SMEM)] + [vmem] * 8,
        out_specs=(vmem, vmem),
        scratch_shapes=[pltpu.VMEM((512, depth), BF)],
        compiler_params=pltpu.CompilerParams(vmem_limit_bytes=8 * 1024 * 1024),
        cost_estimate=pl.CostEstimate(flops=0, bytes_accessed=4 * 512 * depth, transcendentals=0),
        name="arrange",
    )(place, *blocks)


def rotate_here_kernel(rows_ref, basis_ref, out_ref):
    for t in range(0, out_ref.shape[1], TILE):
        out_ref[:, t : t + TILE] = dot_t(rows_ref[...], basis_ref[t : t + TILE])


def rotate_here(rows, basis):
    vmem = pl.BlockSpec(memory_space=pltpu.VMEM)
    whole, depth = basis.shape
    return pl.pallas_call(
        rotate_here_kernel,
        out_shape=jax.ShapeDtypeStruct((256, whole), F32),
        in_specs=[vmem] * 2,
        out_specs=vmem,
        compiler_params=pltpu.CompilerParams(vmem_limit_bytes=16 * 1024 * 1024),
        cost_estimate=pl.CostEstimate(flops=512 * depth * whole, bytes_accessed=2 * depth * whole, transcendentals=0),
        name="rotate_here",
    )(rows, basis)


def rotate_away_kernel(part_ref, rows_ref, basis_ref, *out_refs):
    width = out_refs[0].shape[1]
    for t in range(0, part_ref.shape[1], TILE):
        total = part_ref[:, t : t + TILE] + dot_t(rows_ref[...], basis_ref[t : t + TILE])
        out_refs[t // width][:, t % width : t % width + TILE] = total


def rotate_away(part, rows, basis):
    vmem = pl.BlockSpec(memory_space=pltpu.VMEM)
    whole, depth = basis.shape
    return pl.pallas_call(
        rotate_away_kernel,
        out_shape=[jax.ShapeDtypeStruct((256, whole // STREAMS), F32)] * STREAMS,
        in_specs=[vmem] * 3,
        out_specs=[vmem] * STREAMS,
        compiler_params=pltpu.CompilerParams(vmem_limit_bytes=20 * 1024 * 1024),
        cost_estimate=pl.CostEstimate(flops=512 * depth * whole, bytes_accessed=2 * depth * whole, transcendentals=0),
        name="rotate_away",
    )(part, rows, basis)


def shards(activations, out_grads, act_basis, grad_basis):
    mp, dp = lax.axis_index("mp"), lax.axis_index("dp")
    c, z, h = mp % 2, (mp // 2) % 8, mp // 16
    y, l = dp // 2, dp % 2
    place = jnp.stack([z, c, y, l, h]).astype(jnp.int32)

    pair = cat(out_grads, swap(out_grads, "out_grads_pair"))

    def shift(x, b):
        with jax.named_scope(f"activations_{b}"):
            return lax.ppermute(x, "dp", dp_perm(lambda y, l: (y + b // 2, l + b % 2)))

    blocks = [activations] + [None] * 7
    for b in (4, 2, 6, 1):
        blocks[b] = shift(activations, b)
    basis_away = swap(after(act_basis, pair), "basis_away")
    far = across(pair, "far")
    blocks[3] = shift(blocks[1], 2)
    blocks[7] = shift(blocks[1], 6)
    blocks[5] = shift(blocks[4], 1)
    n0 = cat(pair[:16], far[:16], pair[16:], far[16:])
    n2 = ahead2(n0, "n2")
    x_here, theirs = arrange(place, blocks)
    x_away = swap(theirs, "x_away")
    part = rotate_here(x_here, act_basis)
    n02 = cat(n0, n2)
    n13 = ahead(n02, "n13")
    n4 = ahead2(n2[:32], "n4")

    whole = act_basis.shape[0]
    width = whole // STREAMS
    streams = range(STREAMS)
    p = rotate_away(part, x_away, basis_away)

    r = [ahead(p[s][192:224].astype(BF), f"step1_{s}") for s in streams]
    near = after(cat(n2, n13, n4), p[0])
    g = rotate_grads(place, n0, near, swap(near, "near_away"), grad_basis)
    g_away = lax.ppermute(g, "dp", Y1)
    r = [cat(p[s][128:160] + r[s].astype(F32), p[s][160:192]).astype(BF) for s in streams]
    r = [ahead(r[s], f"step2_{s}") for s in streams]
    r[0] = after(r[0], g)
    r = [ahead((p[s][64:128] + r[s].astype(F32)).astype(BF), f"step3_{s}") for s in streams]
    r = [ahead((p[s][0:64] + r[s].astype(F32)).astype(BF), f"step4_{s}") for s in streams]
    g = g + g_away
    g_away = lax.ppermute(g, "dp", Y2)
    r[1] = after(r[1], g)
    r = [p[s][224:256] + r[s][:32].astype(F32) + swap(r[s][32:], f"other_{s}").astype(F32) for s in streams]
    own = [(r[s] + across(r[s].astype(BF), f"across_{s}").astype(F32)).astype(BF) for s in streams]

    twin = [swap(own[s], f"twin_{s}") for s in streams]
    a1 = [ahead(cat(own[s], twin[s]), f"a1_{s}") for s in streams]
    g = g + g_away
    g_away = lax.ppermute(g, "dp", XLO)
    a1[0] = after(a1[0], g)
    a2 = [ahead(a1[s], f"a2_{s}") for s in streams]
    b12 = [swap(cat(a1[s], a2[s]), f"b12_{s}") for s in streams]
    a3 = [ahead(a2[s], f"a3_{s}") for s in streams]
    g = (g + g_away).astype(BF)
    a4 = [ahead(after(a3[s][:32], g), f"a4_{s}") for s in streams]
    b34 = [swap(cat(a3[s], a4[s]), f"b34_{s}") for s in streams]
    out = None
    for s in streams:
        parts = [x[s] for x in (own, twin, a1, a2, a3, a4, b12, b34)]
        out = finish(place, g, parts, width, s * width, whole, out)
    return out


def solution(mesh):
    return jax.shard_map(
        shards,
        mesh=mesh,
        in_specs=(P("dp", "mp"), P("mp", "dp"), P("dp", "mp"), P("mp", "dp")),
        out_specs=P("mp", "dp"),
        check_vma=False,
    )
```

profile of v0, /device:TPU:1, one launch (start us, length us, event | category | flops | bytes accessed | tf_op | source)
XLA Modules:
  0.0 122.1 jit_solution(13351219195632919241)
XLA Ops:
  0.0 3.2 %collective-permute-start = (bf16[16,1024]{1,0:T(8,128)(2,1)}, bf16[16,1024]{1,0:T(8,128)(2,1)S(1)}, u32[]{:S(2)}, u32[]{:S(2)}) collective-permute-start(bf16[16,1024]{1,0:T(8,128)(2,1)} %param.5), channel_id=1, source_target_pairs={{0,1},{1,0},{2,3},{3,2},{4,5},{5,4},{6,7},{7,6},{8,9},{9,8},{10,11... | collective-permute-start | bytes 98312 | tf_op jit(solution)/shard_map/out_grads_pair/ppermute | solution.py:43
  6.0 2.9 %collective-permute-start.8 = (bf16[64,896]{1,0:T(8,128)(2,1)}, bf16[64,896]{1,0:T(8,128)(2,1)S(1)}, u32[]{:S(2)}, u32[]{:S(2)}) collective-permute-start(bf16[64,896]{1,0:T(8,128)(2,1)} %refs_0_.1), channel_id=1, source_target_pairs={{0,128},{32,160},{64,192},{96,224},{128,0},{160,32},{192,64},{224,... | collective-permute-start | bytes 344072 | tf_op jit(solution)/shard_map/activations_4/ppermute | solution.py:249
  11.2 6.1 %collective-permute-start.2 = (bf16[64,1024]{1,0:T(8,128)(2,1)S(1)}, bf16[64,1024]{1,0:T(8,128)(2,1)S(1)}, u32[]{:S(2)}, u32[]{:S(2)}) collective-permute-start(bf16[64,1024]{1,0:T(8,128)(2,1)S(1)} %pad_maximum_fusion.9.n0_ref), channel_id=1, source_target_pairs={{0,4},{1,13},{2,6},{3,15},{4,8},{5,1},{6,10},{7,3},{8,12},{9,5},{1... | collective-permute-start | bytes 393224 | tf_op jit(solution)/shard_map/n2/ppermute | solution.py:53
  17.3 2.0 %collective-permute-start.11 = (bf16[64,896]{1,0:T(8,128)(2,1)S(1)}, bf16[64,896]{1,0:T(8,128)(2,1)S(1)}, u32[]{:S(2)}, u32[]{:S(2)}) collective-permute-start(bf16[64,896]{1,0:T(8,128)(2,1)S(1)} %collective-permute-done.5.refs_1_), channel_id=1, source_target_pairs={{0,192},{32,224},{64,0},{96,32},{128,64},{160,96},{192,128},{224,1... | collective-permute-start | bytes 344072 | tf_op jit(solution)/shard_map/activations_6/ppermute | solution.py:249
  21.7 3.2 %collective-permute-done.7.refs_3_ = bf16[64,896]{1,0:T(8,128)(2,1)S(1)} collective-permute-done((bf16[64,896]{1,0:T(8,128)(2,1)S(1)}, bf16[64,896]{1,0:T(8,128)(2,1)S(1)}, u32[]{:S(2)}, u32[]{:S(2)}) %collective-permute-start.7) | collective-permute-done | bytes 114720 | tf_op jit(solution)/shard_map/activations_2/ppermute | solution.py:249
  27.0 3.9 %collective-permute-start.3 = (bf16[128,1024]{1,0:T(8,128)(2,1)S(1)}, bf16[128,1024]{1,0:T(8,128)(2,1)S(1)}, u32[]{:S(2)}, u32[]{:S(2)}) collective-permute-start(bf16[128,1024]{1,0:T(8,128)(2,1)S(1)} %constant_dynamic-update-slice_fusion.2), channel_id=1, source_target_pairs={{0,2},{1,15},{2,4},{3,1},{4,6},{5,3},{6,8},{7,5},{8,10},{9,7},{10,... | collective-permute-start | bytes 786440 | tf_op jit(solution)/shard_map/n13/ppermute | solution.py:48
  32.0 2.8 %copy-done = bf16[3584,896]{1,0:T(8,128)(2,1)S(1)} copy-done((bf16[3584,896]{1,0:T(8,128)(2,1)S(1)}, bf16[3584,896]{1,0:T(8,128)(2,1)}, u32[]{:S(2)}) %copy-start) | copy-done | bytes 6422552
  34.9 2.1 %rotate_here.1.part_ref = f32[256,3584]{1,0:T(8,128)S(1)} custom-call(bf16[256,896]{1,0:T(8,128)(2,1)S(1)} %get-tuple-element.16.rows_ref, bf16[3584,896]{1,0:T(8,128)(2,1)S(1)} %copy-done), custom_call_target="tpu_custom_call" | custom-call | flops 1644167168 | bytes 6422528 | tf_op jit(solution)/shard_map/rotate_here/pallas_call | solution.py:207
  37.0 4.9 %rotate_away.1 = (f32[256,1792]{1,0:T(8,128)S(1)}, f32[256,1792]{1,0:T(8,128)S(1)}) custom-call(f32[256,3584]{1,0:T(8,128)S(1)} %rotate_here.1.part_ref, bf16[256,896]{1,0:T(8,128)(2,1)S(1)} %collective-permute-done.12.rows_ref, bf16[3584,896]{1,0:T(8,128)(2,1)} %collective-permute-done.13.basis_ref), custom_call_target="tpu_custom_call" | custom-call | flops 1644167168 | bytes 6422528 | tf_op jit(solution)/shard_map/rotate_away/pallas_call | solution.py:228
  43.9 2.7 %collective-permute-start.18 = (bf16[32,1792]{1,0:T(8,128)(2,1)S(1)}, bf16[32,1792]{1,0:T(8,128)(2,1)S(1)}, u32[]{:S(2)}, u32[]{:S(2)}) collective-permute-start(bf16[32,1792]{1,0:T(8,128)(2,1)S(1)} %get-tuple-element.29), channel_id=1, source_target_pairs={{0,2},{1,15},{2,4},{3,1},{4,6},{5,3},{6,8},{7,5},{8,10},{9,7},{10,... | collective-permute-start | bytes 344072 | tf_op jit(solution)/shard_map/step1_1/ppermute | solution.py:48
  46.6 1.7 %collective-permute-start.32 = (bf16[64,1792]{1,0:T(8,128)(2,1)S(1)}, bf16[64,1792]{1,0:T(8,128)(2,1)S(1)}, u32[]{:S(2)}, u32[]{:S(2)}) collective-permute-start(bf16[64,1792]{1,0:T(8,128)(2,1)S(1)} %pad_maximum_fusion.7), channel_id=1, source_target_pairs={{0,2},{1,15},{2,4},{3,1},{4,6},{5,3},{6,8},{7,5},{8,10},{9,7},{10,... | collective-permute-start | bytes 688136 | tf_op jit(solution)/shard_map/step2_0/ppermute | solution.py:48
  48.4 3.1 %collective-permute-start.19 = (bf16[64,1792]{1,0:T(8,128)(2,1)S(1)}, bf16[64,1792]{1,0:T(8,128)(2,1)S(1)}, u32[]{:S(2)}, u32[]{:S(2)}) collective-permute-start(bf16[64,1792]{1,0:T(8,128)(2,1)S(1)} %pad_maximum_fusion.5), channel_id=1, source_target_pairs={{0,2},{1,15},{2,4},{3,1},{4,6},{5,3},{6,8},{7,5},{8,10},{9,7},{10,... | collective-permute-start | bytes 688136 | tf_op jit(solution)/shard_map/step2_1/ppermute | solution.py:48
  52.7 1.8 %collective-permute-start.33 = (bf16[64,1792]{1,0:T(8,128)(2,1)S(1)}, bf16[64,1792]{1,0:T(8,128)(2,1)S(1)}, u32[]{:S(2)}, u32[]{:S(2)}) collective-permute-start(bf16[64,1792]{1,0:T(8,128)(2,1)S(1)} %add_convert_fusion.2), channel_id=1, source_target_pairs={{0,2},{1,15},{2,4},{3,1},{4,6},{5,3},{6,8},{7,5},{8,10},{9,7},{10,... | collective-permute-start | bytes 688136 | tf_op jit(solution)/shard_map/step3_0/ppermute | solution.py:48
  54.6 3.2 %collective-permute-start.20 = (bf16[64,1792]{1,0:T(8,128)(2,1)S(1)}, bf16[64,1792]{1,0:T(8,128)(2,1)S(1)}, u32[]{:S(2)}, u32[]{:S(2)}) collective-permute-start(bf16[64,1792]{1,0:T(8,128)(2,1)S(1)} %add_convert_fusion.4), channel_id=1, source_target_pairs={{0,2},{1,15},{2,4},{3,1},{4,6},{5,3},{6,8},{7,5},{8,10},{9,7},{10,... | collective-permute-start | bytes 688136 | tf_op jit(solution)/shard_map/step3_1/ppermute | solution.py:48
  58.0 2.7 %collective-permute-start.34 = (bf16[64,1792]{1,0:T(8,128)(2,1)S(1)}, bf16[64,1792]{1,0:T(8,128)(2,1)S(1)}, u32[]{:S(2)}, u32[]{:S(2)}) collective-permute-start(bf16[64,1792]{1,0:T(8,128)(2,1)S(1)} %add_convert_fusion.1), channel_id=1, source_target_pairs={{0,2},{1,15},{2,4},{3,1},{4,6},{5,3},{6,8},{7,5},{8,10},{9,7},{10,... | collective-permute-start | bytes 688136 | tf_op jit(solution)/shard_map/step4_0/ppermute | solution.py:48
  60.8 3.2 %collective-permute-start.21 = (bf16[64,1792]{1,0:T(8,128)(2,1)S(1)}, bf16[64,1792]{1,0:T(8,128)(2,1)S(1)}, u32[]{:S(2)}, u32[]{:S(2)}) collective-permute-start(bf16[64,1792]{1,0:T(8,128)(2,1)S(1)} %add_convert_fusion.3), channel_id=1, source_target_pairs={{0,2},{1,15},{2,4},{3,1},{4,6},{5,3},{6,8},{7,5},{8,10},{9,7},{10,... | collective-permute-start | bytes 688136 | tf_op jit(solution)/shard_map/step4_1/ppermute | solution.py:48
  64.0 7.6 %collective-permute-start.35 = (bf16[32,1792]{1,0:T(8,128)(2,1)S(1)}, bf16[32,1792]{1,0:T(8,128)(2,1)S(1)}, u32[]{:S(2)}, u32[]{:S(2)}) collective-permute-start(bf16[32,1792]{1,0:T(8,128)(2,1)S(1)} %slice.97), channel_id=1, source_target_pairs={{0,1},{1,0},{2,3},{3,2},{4,5},{5,4},{6,7},{7,6},{8,9},{9,8},{10,11... | collective-permute-start | bytes 344072 | tf_op jit(solution)/shard_map/other_0/ppermute | solution.py:43
  71.7 1.5 %collective-permute-start.16 = (f32[256,512]{1,0:T(8,128)S(1)}, f32[256,512]{1,0:T(8,128)S(1)}, u32[]{:S(2)}, u32[]{:S(2)}) collective-permute-start(f32[256,512]{1,0:T(8,128)S(1)} %add.61), channel_id=1, source_target_pairs={{0,128},{32,160},{64,192},{96,224},{128,0},{160,32},{192,64},{224,... | collective-permute-start | bytes 1572872 | tf_op jit(solution)/shard_map/ppermute | solution.py:283
  74.4 1.8 %collective-permute-start.36 = (bf16[32,1792]{1,0:T(8,128)(2,1)S(1)}, bf16[32,1792]{1,0:T(8,128)(2,1)S(1)}, u32[]{:S(2)}, u32[]{:S(2)}) collective-permute-start(bf16[32,1792]{1,0:T(8,128)(2,1)S(1)} %fusion.1), channel_id=1, source_target_pairs={{0,16},{1,17},{2,18},{3,19},{4,20},{5,21},{6,22},{7,23},{8,24},{9,... | collective-permute-start | bytes 344072 | tf_op jit(solution)/shard_map/across_0/ppermute | solution.py:58
  77.6 3.2 %collective-permute-done.36 = bf16[32,1792]{1,0:T(8,128)(2,1)S(1)} collective-permute-done((bf16[32,1792]{1,0:T(8,128)(2,1)S(1)}, bf16[32,1792]{1,0:T(8,128)(2,1)S(1)}, u32[]{:S(2)}, u32[]{:S(2)}) %collective-permute-start.36) | collective-permute-done | bytes 114720 | tf_op jit(solution)/shard_map/across_0/ppermute | solution.py:58
  84.4 2.1 %collective-permute-done.16 = f32[256,512]{1,0:T(8,128)S(1)} collective-permute-done((f32[256,512]{1,0:T(8,128)S(1)}, f32[256,512]{1,0:T(8,128)S(1)}, u32[]{:S(2)}, u32[]{:S(2)}) %collective-permute-start.16) | collective-permute-done | bytes 524320 | tf_op jit(solution)/shard_map/ppermute | solution.py:283
  87.9 1.5 %collective-permute-done.38.refs_2_ = bf16[64,1792]{1,0:T(8,128)(2,1)S(1)} collective-permute-done((bf16[64,1792]{1,0:T(8,128)(2,1)S(1)}, bf16[64,1792]{1,0:T(8,128)(2,1)S(1)}, u32[]{:S(2)}, u32[]{:S(2)}) %collective-permute-start.38) | collective-permute-done | bytes 229408 | tf_op jit(solution)/shard_map/a1_0/ppermute | solution.py:48
  90.4 2.6 %collective-permute-done.25.refs_2_ = bf16[64,1792]{1,0:T(8,128)(2,1)S(1)} collective-permute-done((bf16[64,1792]{1,0:T(8,128)(2,1)S(1)}, bf16[64,1792]{1,0:T(8,128)(2,1)S(1)}, u32[]{:S(2)}, u32[]{:S(2)}) %collective-permute-start.25) | collective-permute-done | bytes 229408 | tf_op jit(solution)/shard_map/a1_1/ppermute | solution.py:48
  94.0 1.5 %collective-permute-done.39.refs_3_ = bf16[64,1792]{1,0:T(8,128)(2,1)S(1)} collective-permute-done((bf16[64,1792]{1,0:T(8,128)(2,1)S(1)}, bf16[64,1792]{1,0:T(8,128)(2,1)S(1)}, u32[]{:S(2)}, u32[]{:S(2)}) %collective-permute-start.39) | collective-permute-done | bytes 229408 | tf_op jit(solution)/shard_map/a2_0/ppermute | solution.py:48
  96.6 2.8 %collective-permute-start.42 = (bf16[128,1792]{1,0:T(8,128)(2,1)S(1)}, bf16[128,1792]{1,0:T(8,128)(2,1)S(1)}, u32[]{:S(2)}, u32[]{:S(2)}) collective-permute-start(bf16[128,1792]{1,0:T(8,128)(2,1)S(1)} %pad_maximum_fusion.2), channel_id=1, source_target_pairs={{0,1},{1,0},{2,3},{3,2},{4,5},{5,4},{6,7},{7,6},{8,9},{9,8},{10,11... | collective-permute-start | bytes 1376264 | tf_op jit(solution)/shard_map/b12_0/ppermute | solution.py:43
  99.4 3.0 %collective-permute-start.27 = (bf16[64,1792]{1,0:T(8,128)(2,1)S(1)}, bf16[64,1792]{1,0:T(8,128)(2,1)S(1)}, u32[]{:S(2)}, u32[]{:S(2)}) collective-permute-start(bf16[64,1792]{1,0:T(8,128)(2,1)S(1)} %collective-permute-done.26.refs_3_), channel_id=1, source_target_pairs={{0,2},{1,15},{2,4},{3,1},{4,6},{5,3},{6,8},{7,5},{8,10},{9,7},{10,... | collective-permute-start | bytes 688136 | tf_op jit(solution)/shard_map/a3_1/ppermute | solution.py:48
  102.8 4.0 %collective-permute-start.29 = (bf16[128,1792]{1,0:T(8,128)(2,1)S(1)}, bf16[128,1792]{1,0:T(8,128)(2,1)S(1)}, u32[]{:S(2)}, u32[]{:S(2)}) collective-permute-start(bf16[128,1792]{1,0:T(8,128)(2,1)S(1)} %pad_maximum_fusion.1), channel_id=1, source_target_pairs={{0,1},{1,0},{2,3},{3,2},{4,5},{5,4},{6,7},{7,6},{8,9},{9,8},{10,11... | collective-permute-start | bytes 1376264 | tf_op jit(solution)/shard_map/b12_1/ppermute | solution.py:43
  106.8 3.0 %collective-permute-start.28 = (bf16[32,1792]{1,0:T(8,128)(2,1)S(1)}, bf16[32,1792]{1,0:T(8,128)(2,1)S(1)}, u32[]{:S(2)}, u32[]{:S(2)}) collective-permute-start(bf16[32,1792]{1,0:T(8,128)(2,1)S(1)} %slice.93), channel_id=1, source_target_pairs={{0,2},{1,15},{2,4},{3,1},{4,6},{5,3},{6,8},{7,5},{8,10},{9,7},{10,... | collective-permute-start | bytes 344072 | tf_op jit(solution)/shard_map/a4_1/ppermute | solution.py:48
  109.9 2.9 %collective-permute-start.43 = (bf16[96,1792]{1,0:T(8,128)(2,1)S(1)}, bf16[96,1792]{1,0:T(8,128)(2,1)S(1)}, u32[]{:S(2)}, u32[]{:S(2)}) collective-permute-start(bf16[96,1792]{1,0:T(8,128)(2,1)S(1)} %pad_maximum_fusion.4), channel_id=1, source_target_pairs={{0,1},{1,0},{2,3},{3,2},{4,5},{5,4},{6,7},{7,6},{8,9},{9,8},{10,11... | collective-permute-start | bytes 1032200 | tf_op jit(solution)/shard_map/b34_0/ppermute | solution.py:43
  112.8 4.6 %collective-permute-start.30 = (bf16[96,1792]{1,0:T(8,128)(2,1)S(1)}, bf16[96,1792]{1,0:T(8,128)(2,1)S(1)}, u32[]{:S(2)}, u32[]{:S(2)}) collective-permute-start(bf16[96,1792]{1,0:T(8,128)(2,1)S(1)} %pad_maximum_fusion.3), channel_id=1, source_target_pairs={{0,1},{1,0},{2,3},{3,2},{4,5},{5,4},{6,7},{7,6},{8,9},{9,8},{10,11... | collective-permute-start | bytes 1032200 | tf_op jit(solution)/shard_map/b34_1/ppermute | solution.py:43
  117.4 2.2 %finish.2.refs_8_ = f32[256,3584]{1,0:T(8,128)} custom-call(s32[5]{0:T(128)S(1)} %stack.23.place_ref, bf16[256,512]{1,0:T(8,128)(2,1)S(1)} %add_convert_fusion.g_ref, bf16[32,1792]{1,0:T(8,128)(2,1)S(1)} %add_convert_fusion.5.refs_0_, bf16[32,1792]{1,0:T(8,128)(2,1)S(1)} %collective-permute-done.37.refs_1_, ...), custom_call_target="tpu_custom_call" | custom-call | flops 469762048 | bytes 3670016 | tf_op jit(solution)/shard_map/finish/pallas_call | solution.py:114
  119.7 2.2 %finish.3 = f32[256,3584]{1,0:T(8,128)} custom-call(s32[5]{0:T(128)S(1)} %stack.23.place_ref, bf16[256,512]{1,0:T(8,128)(2,1)S(1)} %add_convert_fusion.g_ref, bf16[32,1792]{1,0:T(8,128)(2,1)S(1)} %add_convert_fusion.7.refs_0_, bf16[32,1792]{1,0:T(8,128)(2,1)S(1)} %collective-permute-done.24.refs_1_, ...), custom_call_target="tpu_custom_call", output_to_operand_aliasing={{}: (10, {})} | custom-call | flops 469762048 | bytes 3670016 | tf_op jit(solution)/shard_map/finish/pallas_call | solution.py:114
  (107 shorter events, 25.5 us)
Async XLA Ops:
  4.3 32.7 %collective-permute-start.13 = (bf16[3584,896]{1,0:T(8,128)(2,1)}, bf16[3584,896]{1,0:T(8,128)(2,1)}, u32[]{:S(2)}, u32[]{:S(2)}) collective-permute-start(bf16[3584,896]{1,0:T(8,128)(2,1)} %basis_ref.2), channel_id=1, source_target_pairs={{0,1},{1,0},{2,3},{3,2},{4,5},{5,4},{6,7},{7,6},{8,9},{9,8},{10,11... | collective-permute-start | bytes 19267592 | tf_op jit(solution)/shard_map/basis_away/ppermute | solution.py:43
  6.0 11.3 %collective-permute-start.8 = (bf16[64,896]{1,0:T(8,128)(2,1)}, bf16[64,896]{1,0:T(8,128)(2,1)S(1)}, u32[]{:S(2)}, u32[]{:S(2)}) collective-permute-start(bf16[64,896]{1,0:T(8,128)(2,1)} %refs_0_.1), channel_id=1, source_target_pairs={{0,128},{32,160},{64,192},{96,224},{128,0},{160,32},{192,64},{224,... | collective-permute-start | bytes 344072 | tf_op jit(solution)/shard_map/activations_4/ppermute | solution.py:249
  8.9 10.4 %collective-permute-start.10 = (bf16[64,896]{1,0:T(8,128)(2,1)}, bf16[64,896]{1,0:T(8,128)(2,1)S(1)}, u32[]{:S(2)}, u32[]{:S(2)}) collective-permute-start(bf16[64,896]{1,0:T(8,128)(2,1)} %refs_0_.1), channel_id=1, source_target_pairs={{0,192},{32,224},{64,0},{96,32},{128,64},{160,96},{192,128},{224,1... | collective-permute-start | bytes 344072 | tf_op jit(solution)/shard_map/activations_6/ppermute | solution.py:249
  9.7 9.6 %collective-permute-start.6 = (bf16[64,896]{1,0:T(8,128)(2,1)}, bf16[64,896]{1,0:T(8,128)(2,1)S(1)}, u32[]{:S(2)}, u32[]{:S(2)}) collective-permute-start(bf16[64,896]{1,0:T(8,128)(2,1)} %refs_0_.1), channel_id=1, source_target_pairs={{0,64},{32,96},{64,128},{96,160},{128,192},{160,224},{192,0},{224,... | collective-permute-start | bytes 344072 | tf_op jit(solution)/shard_map/activations_2/ppermute | solution.py:249
  11.2 15.8 %collective-permute-start.2 = (bf16[64,1024]{1,0:T(8,128)(2,1)S(1)}, bf16[64,1024]{1,0:T(8,128)(2,1)S(1)}, u32[]{:S(2)}, u32[]{:S(2)}) collective-permute-start(bf16[64,1024]{1,0:T(8,128)(2,1)S(1)} %pad_maximum_fusion.9.n0_ref), channel_id=1, source_target_pairs={{0,4},{1,13},{2,6},{3,15},{4,8},{5,1},{6,10},{7,3},{8,12},{9,5},{1... | collective-permute-start | bytes 393224 | tf_op jit(solution)/shard_map/n2/ppermute | solution.py:53
  19.3 5.6 %collective-permute-start.7 = (bf16[64,896]{1,0:T(8,128)(2,1)S(1)}, bf16[64,896]{1,0:T(8,128)(2,1)S(1)}, u32[]{:S(2)}, u32[]{:S(2)}) collective-permute-start(bf16[64,896]{1,0:T(8,128)(2,1)S(1)} %collective-permute-done.5.refs_1_), channel_id=1, source_target_pairs={{0,64},{32,96},{64,128},{96,160},{128,192},{160,224},{192,0},{224,... | collective-permute-start | bytes 344072 | tf_op jit(solution)/shard_map/activations_2/ppermute | solution.py:249
  19.3 5.6 %collective-permute-start.9 = (bf16[64,896]{1,0:T(8,128)(2,1)S(1)}, bf16[64,896]{1,0:T(8,128)(2,1)S(1)}, u32[]{:S(2)}, u32[]{:S(2)}) collective-permute-start(bf16[64,896]{1,0:T(8,128)(2,1)S(1)} %collective-permute-done.8.refs_4_), channel_id=1, source_target_pairs={{0,32},{32,0},{64,96},{96,64},{128,160},{160,128},{192,224},{224,1... | collective-permute-start | bytes 344072 | tf_op jit(solution)/shard_map/activations_1/ppermute | solution.py:249
  26.5 10.5 %collective-permute-start.12 = (bf16[256,896]{1,0:T(8,128)(2,1)S(1)}, bf16[256,896]{1,0:T(8,128)(2,1)S(1)}, u32[]{:S(2)}, u32[]{:S(2)}) collective-permute-start(bf16[256,896]{1,0:T(8,128)(2,1)S(1)} %get-tuple-element.17), channel_id=1, source_target_pairs={{0,1},{1,0},{2,3},{3,2},{4,5},{5,4},{6,7},{7,6},{8,9},{9,8},{10,11... | collective-permute-start | bytes 1376264 | tf_op jit(solution)/shard_map/x_away/ppermute | solution.py:43
  27.0 10.0 %collective-permute-start.3 = (bf16[128,1024]{1,0:T(8,128)(2,1)S(1)}, bf16[128,1024]{1,0:T(8,128)(2,1)S(1)}, u32[]{:S(2)}, u32[]{:S(2)}) collective-permute-start(bf16[128,1024]{1,0:T(8,128)(2,1)S(1)} %constant_dynamic-update-slice_fusion.2), channel_id=1, source_target_pairs={{0,2},{1,15},{2,4},{3,1},{4,6},{5,3},{6,8},{7,5},{8,10},{9,7},{10,... | collective-permute-start | bytes 786440 | tf_op jit(solution)/shard_map/n13/ppermute | solution.py:48
  30.9 6.1 %collective-permute-start.4 = (bf16[32,1024]{1,0:T(8,128)(2,1)S(1)}, bf16[32,1024]{1,0:T(8,128)(2,1)S(1)}, u32[]{:S(2)}, u32[]{:S(2)}) collective-permute-start(bf16[32,1024]{1,0:T(8,128)(2,1)S(1)} %slice.90), channel_id=1, source_target_pairs={{0,4},{1,13},{2,6},{3,15},{4,8},{5,1},{6,10},{7,3},{8,12},{9,5},{1... | collective-permute-start | bytes 196616 | tf_op jit(solution)/shard_map/n4/ppermute | solution.py:53
  43.3 8.2 %collective-permute-start.14 = (bf16[224,1024]{1,0:T(8,128)(2,1)S(1)}, bf16[224,1024]{1,0:T(8,128)(2,1)S(1)}, u32[]{:S(2)}, u32[]{:S(2)}) collective-permute-start(bf16[224,1024]{1,0:T(8,128)(2,1)S(1)} %pad_maximum_fusion.near_ref), channel_id=1, source_target_pairs={{0,1},{1,0},{2,3},{3,2},{4,5},{5,4},{6,7},{7,6},{8,9},{9,8},{10,11... | collective-permute-start | bytes 1376264 | tf_op jit(solution)/shard_map/near_away/ppermute | solution.py:43
  46.6 6.0 %collective-permute-start.32 = (bf16[64,1792]{1,0:T(8,128)(2,1)S(1)}, bf16[64,1792]{1,0:T(8,128)(2,1)S(1)}, u32[]{:S(2)}, u32[]{:S(2)}) collective-permute-start(bf16[64,1792]{1,0:T(8,128)(2,1)S(1)} %pad_maximum_fusion.7), channel_id=1, source_target_pairs={{0,2},{1,15},{2,4},{3,1},{4,6},{5,3},{6,8},{7,5},{8,10},{9,7},{10,... | collective-permute-start | bytes 688136 | tf_op jit(solution)/shard_map/step2_0/ppermute | solution.py:48
  48.4 6.1 %collective-permute-start.19 = (bf16[64,1792]{1,0:T(8,128)(2,1)S(1)}, bf16[64,1792]{1,0:T(8,128)(2,1)S(1)}, u32[]{:S(2)}, u32[]{:S(2)}) collective-permute-start(bf16[64,1792]{1,0:T(8,128)(2,1)S(1)} %pad_maximum_fusion.5), channel_id=1, source_target_pairs={{0,2},{1,15},{2,4},{3,1},{4,6},{5,3},{6,8},{7,5},{8,10},{9,7},{10,... | collective-permute-start | bytes 688136 | tf_op jit(solution)/shard_map/step2_1/ppermute | solution.py:48
  54.6 6.2 %collective-permute-start.20 = (bf16[64,1792]{1,0:T(8,128)(2,1)S(1)}, bf16[64,1792]{1,0:T(8,128)(2,1)S(1)}, u32[]{:S(2)}, u32[]{:S(2)}) collective-permute-start(bf16[64,1792]{1,0:T(8,128)(2,1)S(1)} %add_convert_fusion.4), channel_id=1, source_target_pairs={{0,2},{1,15},{2,4},{3,1},{4,6},{5,3},{6,8},{7,5},{8,10},{9,7},{10,... | collective-permute-start | bytes 688136 | tf_op jit(solution)/shard_map/step3_1/ppermute | solution.py:48
  57.8 13.8 %collective-permute-start.15 = (f32[256,512]{1,0:T(8,128)S(1)}, f32[256,512]{1,0:T(8,128)S(1)}, u32[]{:S(2)}, u32[]{:S(2)}) collective-permute-start(f32[256,512]{1,0:T(8,128)S(1)} %rotate_grads.1), channel_id=1, source_target_pairs={{0,64},{32,96},{64,0},{96,32},{128,192},{160,224},{192,128},{224,1... | collective-permute-start | bytes 1572872 | tf_op jit(solution)/shard_map/ppermute | solution.py:276
  58.0 6.0 %collective-permute-start.34 = (bf16[64,1792]{1,0:T(8,128)(2,1)S(1)}, bf16[64,1792]{1,0:T(8,128)(2,1)S(1)}, u32[]{:S(2)}, u32[]{:S(2)}) collective-permute-start(bf16[64,1792]{1,0:T(8,128)(2,1)S(1)} %add_convert_fusion.1), channel_id=1, source_target_pairs={{0,2},{1,15},{2,4},{3,1},{4,6},{5,3},{6,8},{7,5},{8,10},{9,7},{10,... | collective-permute-start | bytes 688136 | tf_op jit(solution)/shard_map/step4_0/ppermute | solution.py:48
  60.8 12.4 %collective-permute-start.21 = (bf16[64,1792]{1,0:T(8,128)(2,1)S(1)}, bf16[64,1792]{1,0:T(8,128)(2,1)S(1)}, u32[]{:S(2)}, u32[]{:S(2)}) collective-permute-start(bf16[64,1792]{1,0:T(8,128)(2,1)S(1)} %add_convert_fusion.3), channel_id=1, source_target_pairs={{0,2},{1,15},{2,4},{3,1},{4,6},{5,3},{6,8},{7,5},{8,10},{9,7},{10,... | collective-permute-start | bytes 688136 | tf_op jit(solution)/shard_map/step4_1/ppermute | solution.py:48
  64.0 10.3 %collective-permute-start.35 = (bf16[32,1792]{1,0:T(8,128)(2,1)S(1)}, bf16[32,1792]{1,0:T(8,128)(2,1)S(1)}, u32[]{:S(2)}, u32[]{:S(2)}) collective-permute-start(bf16[32,1792]{1,0:T(8,128)(2,1)S(1)} %slice.97), channel_id=1, source_target_pairs={{0,1},{1,0},{2,3},{3,2},{4,5},{5,4},{6,7},{7,6},{8,9},{9,8},{10,11... | collective-permute-start | bytes 344072 | tf_op jit(solution)/shard_map/other_0/ppermute | solution.py:43
  71.7 14.8 %collective-permute-start.16 = (f32[256,512]{1,0:T(8,128)S(1)}, f32[256,512]{1,0:T(8,128)S(1)}, u32[]{:S(2)}, u32[]{:S(2)}) collective-permute-start(f32[256,512]{1,0:T(8,128)S(1)} %add.61), channel_id=1, source_target_pairs={{0,128},{32,160},{64,192},{96,224},{128,0},{160,32},{192,64},{224,... | collective-permute-start | bytes 1572872 | tf_op jit(solution)/shard_map/ppermute | solution.py:283
  74.4 6.4 %collective-permute-start.36 = (bf16[32,1792]{1,0:T(8,128)(2,1)S(1)}, bf16[32,1792]{1,0:T(8,128)(2,1)S(1)}, u32[]{:S(2)}, u32[]{:S(2)}) collective-permute-start(bf16[32,1792]{1,0:T(8,128)(2,1)S(1)} %fusion.1), channel_id=1, source_target_pairs={{0,16},{1,17},{2,18},{3,19},{4,20},{5,21},{6,22},{7,23},{8,24},{9,... | collective-permute-start | bytes 344072 | tf_op jit(solution)/shard_map/across_0/ppermute | solution.py:58
  76.3 6.9 %collective-permute-start.23 = (bf16[32,1792]{1,0:T(8,128)(2,1)S(1)}, bf16[32,1792]{1,0:T(8,128)(2,1)S(1)}, u32[]{:S(2)}, u32[]{:S(2)}) collective-permute-start(bf16[32,1792]{1,0:T(8,128)(2,1)S(1)} %fusion), channel_id=1, source_target_pairs={{0,16},{1,17},{2,18},{3,19},{4,20},{5,21},{6,22},{7,23},{8,24},{9,... | collective-permute-start | bytes 344072 | tf_op jit(solution)/shard_map/across_1/ppermute | solution.py:58
  86.6 15.8 %collective-permute-start.17 = (f32[256,512]{1,0:T(8,128)S(1)}, f32[256,512]{1,0:T(8,128)S(1)}, u32[]{:S(2)}, u32[]{:S(2)}) collective-permute-start(f32[256,512]{1,0:T(8,128)S(1)} %add.62), channel_id=1, source_target_pairs={{0,32},{32,0},{64,96},{96,64},{128,160},{160,128},{192,224},{224,1... | collective-permute-start | bytes 1572872 | tf_op jit(solution)/shard_map/ppermute | solution.py:291
  89.4 6.1 %collective-permute-start.39 = (bf16[64,1792]{1,0:T(8,128)(2,1)S(1)}, bf16[64,1792]{1,0:T(8,128)(2,1)S(1)}, u32[]{:S(2)}, u32[]{:S(2)}) collective-permute-start(bf16[64,1792]{1,0:T(8,128)(2,1)S(1)} %collective-permute-done.38.refs_2_), channel_id=1, source_target_pairs={{0,2},{1,15},{2,4},{3,1},{4,6},{5,3},{6,8},{7,5},{8,10},{9,7},{10,... | collective-permute-start | bytes 688136 | tf_op jit(solution)/shard_map/a2_0/ppermute | solution.py:48
  93.1 6.3 %collective-permute-start.26 = (bf16[64,1792]{1,0:T(8,128)(2,1)S(1)}, bf16[64,1792]{1,0:T(8,128)(2,1)S(1)}, u32[]{:S(2)}, u32[]{:S(2)}) collective-permute-start(bf16[64,1792]{1,0:T(8,128)(2,1)S(1)} %collective-permute-done.25.refs_2_), channel_id=1, source_target_pairs={{0,2},{1,15},{2,4},{3,1},{4,6},{5,3},{6,8},{7,5},{8,10},{9,7},{10,... | collective-permute-start | bytes 688136 | tf_op jit(solution)/shard_map/a2_1/ppermute | solution.py:48
  95.5 6.8 %collective-permute-start.40 = (bf16[64,1792]{1,0:T(8,128)(2,1)S(1)}, bf16[64,1792]{1,0:T(8,128)(2,1)S(1)}, u32[]{:S(2)}, u32[]{:S(2)}) collective-permute-start(bf16[64,1792]{1,0:T(8,128)(2,1)S(1)} %collective-permute-done.39.refs_3_), channel_id=1, source_target_pairs={{0,2},{1,15},{2,4},{3,1},{4,6},{5,3},{6,8},{7,5},{8,10},{9,7},{10,... | collective-permute-start | bytes 688136 | tf_op jit(solution)/shard_map/a3_0/ppermute | solution.py:48
  96.6 20.9 %collective-permute-start.42 = (bf16[128,1792]{1,0:T(8,128)(2,1)S(1)}, bf16[128,1792]{1,0:T(8,128)(2,1)S(1)}, u32[]{:S(2)}, u32[]{:S(2)}) collective-permute-start(bf16[128,1792]{1,0:T(8,128)(2,1)S(1)} %pad_maximum_fusion.2), channel_id=1, source_target_pairs={{0,1},{1,0},{2,3},{3,2},{4,5},{5,4},{6,7},{7,6},{8,9},{9,8},{10,11... | collective-permute-start | bytes 1376264 | tf_op jit(solution)/shard_map/b12_0/ppermute | solution.py:43
  99.4 7.4 %collective-permute-start.27 = (bf16[64,1792]{1,0:T(8,128)(2,1)S(1)}, bf16[64,1792]{1,0:T(8,128)(2,1)S(1)}, u32[]{:S(2)}, u32[]{:S(2)}) collective-permute-start(bf16[64,1792]{1,0:T(8,128)(2,1)S(1)} %collective-permute-done.26.refs_3_), channel_id=1, source_target_pairs={{0,2},{1,15},{2,4},{3,1},{4,6},{5,3},{6,8},{7,5},{8,10},{9,7},{10,... | collective-permute-start | bytes 688136 | tf_op jit(solution)/shard_map/a3_1/ppermute | solution.py:48
  102.4 7.4 %collective-permute-start.41 = (bf16[32,1792]{1,0:T(8,128)(2,1)S(1)}, bf16[32,1792]{1,0:T(8,128)(2,1)S(1)}, u32[]{:S(2)}, u32[]{:S(2)}) collective-permute-start(bf16[32,1792]{1,0:T(8,128)(2,1)S(1)} %slice.98), channel_id=1, source_target_pairs={{0,2},{1,15},{2,4},{3,1},{4,6},{5,3},{6,8},{7,5},{8,10},{9,7},{10,... | collective-permute-start | bytes 344072 | tf_op jit(solution)/shard_map/a4_0/ppermute | solution.py:48
  102.8 16.8 %collective-permute-start.29 = (bf16[128,1792]{1,0:T(8,128)(2,1)S(1)}, bf16[128,1792]{1,0:T(8,128)(2,1)S(1)}, u32[]{:S(2)}, u32[]{:S(2)}) collective-permute-start(bf16[128,1792]{1,0:T(8,128)(2,1)S(1)} %pad_maximum_fusion.1), channel_id=1, source_target_pairs={{0,1},{1,0},{2,3},{3,2},{4,5},{5,4},{6,7},{7,6},{8,9},{9,8},{10,11... | collective-permute-start | bytes 1376264 | tf_op jit(solution)/shard_map/b12_1/ppermute | solution.py:43
  106.8 6.0 %collective-permute-start.28 = (bf16[32,1792]{1,0:T(8,128)(2,1)S(1)}, bf16[32,1792]{1,0:T(8,128)(2,1)S(1)}, u32[]{:S(2)}, u32[]{:S(2)}) collective-permute-start(bf16[32,1792]{1,0:T(8,128)(2,1)S(1)} %slice.93), channel_id=1, source_target_pairs={{0,2},{1,15},{2,4},{3,1},{4,6},{5,3},{6,8},{7,5},{8,10},{9,7},{10,... | collective-permute-start | bytes 344072 | tf_op jit(solution)/shard_map/a4_1/ppermute | solution.py:48
  109.9 7.6 %collective-permute-start.43 = (bf16[96,1792]{1,0:T(8,128)(2,1)S(1)}, bf16[96,1792]{1,0:T(8,128)(2,1)S(1)}, u32[]{:S(2)}, u32[]{:S(2)}) collective-permute-start(bf16[96,1792]{1,0:T(8,128)(2,1)S(1)} %pad_maximum_fusion.4), channel_id=1, source_target_pairs={{0,1},{1,0},{2,3},{3,2},{4,5},{5,4},{6,7},{7,6},{8,9},{9,8},{10,11... | collective-permute-start | bytes 1032200 | tf_op jit(solution)/shard_map/b34_0/ppermute | solution.py:43
  112.8 6.9 %collective-permute-start.30 = (bf16[96,1792]{1,0:T(8,128)(2,1)S(1)}, bf16[96,1792]{1,0:T(8,128)(2,1)S(1)}, u32[]{:S(2)}, u32[]{:S(2)}) collective-permute-start(bf16[96,1792]{1,0:T(8,128)(2,1)S(1)} %pad_maximum_fusion.3), channel_id=1, source_target_pairs={{0,1},{1,0},{2,3},{3,2},{4,5},{5,4},{6,7},{7,6},{8,9},{9,8},{10,11... | collective-permute-start | bytes 1032200 | tf_op jit(solution)/shard_map/b34_1/ppermute | solution.py:43
  (15 other events, 66.3 us)
where the time goes:
time: 122 us
  starting transfers between devices  84.7 us (69%)
  waiting for transfers between devices  17.1 us (14%)
  Pallas kernels  13.3 us (11%)
  local copies, waits for them, and re-layouts  4.67 us (4%)
  other arithmetic  1.86 us (2%)
    ppermute x17, starting transfers between devices, ahead(): return lax.ppermute(x, 'mp', AHEAD)  33 us
    ppermute x12, starting transfers between devices, swap(): return lax.ppermute(x, 'mp', CORE)  29.6 us
    ppermute x7, starting transfers between devices, shift(): return lax.ppermute(x, 'dp', dp_perm(lambda y, l: (y + b // 2, l + b % 2)))  7.91 us
    ppermute x2, starting transfers between devices, ahead2(): return lax.ppermute(x, 'mp', AHEAD2)  7.27 us
    ppermute x17, waiting for transfers between devices, ahead(): return lax.ppermute(x, 'mp', AHEAD)  6.02 us
    pallas_call x1, Pallas kernels, rotate_away(): pl.pallas_call(rotate_away_kernel, out_shape=[jax.ShapeDtypeStruct((256,...  4.91 us
    unnamed x10, local copies, waits for them, and re-layouts  4.5 us
    pallas_call x2, Pallas kernels, finish(): pl.pallas_call(functools.partial(finish_kernel, width, first, int(aliased...  4.44 us
  transfers between devices with their start and end apart: 44, of which 11 were waited for; matrix products, arithmetic and copies ran while one was open for 2% of the time, Pallas kernels for 5%

commit v1 on v0

--- a/solution.py
+++ b/solution.py
@@ -196,44 +196,52 @@
     )(place, *blocks)
 
 
-def rotate_here_kernel(rows_ref, basis_ref, out_ref):
-    for t in range(0, out_ref.shape[1], TILE):
-        out_ref[:, t : t + TILE] = dot_t(rows_ref[...], basis_ref[t : t + TILE])
-
-
-def rotate_here(rows, basis):
-    vmem = pl.BlockSpec(memory_space=pltpu.VMEM)
-    whole, depth = basis.shape
+def rotate_kernel(cuts, here_rows_ref, away_rows_ref, here_ref, away_ref, *refs):
+    out_refs, (here, away, sem) = refs[:STREAMS], refs[STREAMS:]
+    copies = []
+    for i, (lo, hi) in enumerate(zip(cuts, cuts[1:])):
+        rows = pl.ds(lo, hi - lo)
+        copies.append(
+            [
+                pltpu.make_async_copy(ref.at[rows], held.at[rows], sem.at[2 * i + j])
+                for j, (ref, held) in enumerate(((here_ref, here), (away_ref, away)))
+            ]
+        )
+    for pair in copies:
+        for copy in pair:
+            copy.start()
+    width = out_refs[0].shape[1]
+    for pair, lo, hi in zip(copies, cuts, cuts[1:]):
+        for copy in pair:
+            copy.wait()
+        for t in range(lo, hi, TILE):
+            total = dot_t(here_rows_ref[...], here[t : t + TILE]) + dot_t(away_rows_ref[...], away[t : t + TILE])
+            out_refs[t // width][:, t % width : t % width + TILE] = total
+
+
+def rotate(here_rows, away_rows, here, away):
+    vmem, hbm = pl.BlockSpec(memory_space=pltpu.VMEM), pl.BlockSpec(memory_space=pl.ANY)
+    whole, depth = here.shape
+    cuts = list(range(0, whole, 4 * TILE)) + [whole]
     return pl.pallas_call(
-        rotate_here_kernel,
-        out_shape=jax.ShapeDtypeStruct((256, whole), F32),
-        in_specs=[vmem] * 2,
-        out_specs=vmem,
-        compiler_params=pltpu.CompilerParams(vmem_limit_bytes=16 * 1024 * 1024),
-        cost_estimate=pl.CostEstimate(flops=512 * depth * whole, bytes_accessed=2 * depth * whole, transcendentals=0),
-        name="rotate_here",
-    )(rows, basis)
-
-
-def rotate_away_kernel(part_ref, rows_ref, basis_ref, *out_refs):
-    width = out_refs[0].shape[1]
-    for t in range(0, part_ref.shape[1], TILE):
-        total = part_ref[:, t : t + TILE] + dot_t(rows_ref[...], basis_ref[t : t + TILE])
-        out_refs[t // width][:, t % width : t % width + TILE] = total
-
-
-def rotate_away(part, rows, basis):
-    vmem = pl.BlockSpec(memory_space=pltpu.VMEM)
-    whole, depth = basis.shape
-    return pl.pallas_call(
-        rotate_away_kernel,
+        functools.partial(rotate_kernel, cuts),
         out_shape=[jax.ShapeDtypeStruct((256, whole // STREAMS), F32)] * STREAMS,
-        in_specs=[vmem] * 3,
+        in_specs=[vmem, vmem, hbm, hbm],
         out_specs=[vmem] * STREAMS,
-        compiler_params=pltpu.CompilerParams(vmem_limit_bytes=20 * 1024 * 1024),
-        cost_estimate=pl.CostEstimate(flops=512 * depth * whole, bytes_accessed=2 * depth * whole, transcendentals=0),
-        name="rotate_away",
-    )(part, rows, basis)
+        scratch_shapes=[
+            pltpu.VMEM((whole, depth), BF),
+            pltpu.VMEM((whole, depth), BF),
+            pltpu.SemaphoreType.DMA((2 * len(cuts) - 2,)),
+        ],
+        compiler_params=pltpu.CompilerParams(vmem_limit_bytes=24 * 1024 * 1024),
+        cost_estimate=pl.CostEstimate(flops=1024 * depth * whole, bytes_accessed=4 * depth * whole, transcendentals=0),
+        name="rotate",
+    )(
+        here_rows,
+        away_rows,
+        pltpu.with_memory_space_constraint(here, pltpu.HBM),
+        pltpu.with_memory_space_constraint(away, pltpu.HBM),
+    )
 
 
 def shards(activations, out_grads, act_basis, grad_basis):
@@ -259,8 +267,7 @@
     n0 = cat(pair[:16], far[:16], pair[16:], far[16:])
     n2 = ahead2(n0, "n2")
     x_here, theirs = arrange(place, blocks)
-    x_away = swap(theirs, "x_away")
-    part = rotate_here(x_here, act_basis)
+    x_away = swap(after(theirs, n2), "x_away")
     n02 = cat(n0, n2)
     n13 = ahead(n02, "n13")
     n4 = ahead2(n2[:32], "n4")
@@ -268,10 +275,11 @@
     whole = act_basis.shape[0]
     width = whole // STREAMS
     streams = range(STREAMS)
-    p = rotate_away(part, x_away, basis_away)
+    p = rotate(x_here, x_away, act_basis, basis_away)
 
     r = [ahead(p[s][192:224].astype(BF), f"step1_{s}") for s in streams]
-    near = after(cat(n2, n13, n4), p[0])
+    n13, n4 = lax.optimization_barrier((n13, n4, p[0]))[:2]
+    near = cat(n2, n13, n4)
     g = rotate_grads(place, n0, near, swap(near, "near_away"), grad_basis)
     g_away = lax.ppermute(g, "dp", Y1)
     r = [cat(p[s][128:160] + r[s].astype(F32), p[s][160:192]).astype(BF) for s in streams]

time: 122 us -> 118 us (0.967)
  local copies, waits for them, and re-layouts: 4.67 us -> 1.88 us
  starting transfers between devices: 84.7 us -> 82.5 us
    unnamed x10 -> x9, local copies, waits for them, and re-layouts: 4.5 us -> 1.7 us
    ppermute x17, starting transfers between devices: 33 us -> 31.5 us  [ahead(): return lax.ppermute(x, 'mp', AHEAD)]
    ppermute x17, waiting for transfers between devices: 6.02 us -> 7.42 us  [ahead(): return lax.ppermute(x, 'mp', AHEAD)]
    pallas_call x2 -> x1, Pallas kernels: 7 us -> 6.7 us  [rotate(): pl.pallas_call(functools.partial(rotate_kernel, cuts), out_shape=[jax.Sha...]
  transfers between devices with their start and end apart: 44 -> 44, of which waited for: 11 -> 12; matrix products, arithmetic and copies ran while one was open for 2% -> 2% of each run, Pallas kernels for 5% -> 9%
where the time goes in v1:
time: 118 us; the launch traced here: 117 us
  starting transfers between devices  82.5 us (70%)
  waiting for transfers between devices  17.7 us (15%)
  Pallas kernels  13 us (11%)
  local copies, waits for them, and re-layouts  1.88 us (2%)
  other arithmetic  1.82 us (2%)
    ppermute x17, starting transfers between devices, ahead(): return lax.ppermute(x, 'mp', AHEAD)  31.5 us
    ppermute x12, starting transfers between devices, swap(): return lax.ppermute(x, 'mp', CORE)  29.7 us
    ppermute x7, starting transfers between devices, shift(): return lax.ppermute(x, 'dp', dp_perm(lambda y, l: (y + b // 2, l + b % 2)))  7.91 us
    ppermute x17, waiting for transfers between devices, ahead(): return lax.ppermute(x, 'mp', AHEAD)  7.42 us
    ppermute x2, starting transfers between devices, ahead2(): return lax.ppermute(x, 'mp', AHEAD2)  7.27 us
    pallas_call x1, Pallas kernels, rotate(): pl.pallas_call(functools.partial(rotate_kernel, cuts), out_shape=[jax.Sha...  6.7 us
    pallas_call x2, Pallas kernels, finish(): pl.pallas_call(functools.partial(finish_kernel, width, first, int(aliased...  4.44 us
    ppermute x7, waiting for transfers between devices, shift(): return lax.ppermute(x, 'dp', dp_perm(lambda y, l: (y + b // 2, l + b % 2)))  4.3 us
  transfers between devices with their start and end apart: 44, of which 12 were waited for; matrix products, arithmetic and copies ran while one was open for 2% of the time, Pallas kernels for 9%

profile of v1, /device:TPU:1, one launch (start us, length us, event | category | flops | bytes accessed | tf_op | source)
XLA Modules:
  0.0 117.3 jit_solution(2961964965446233249)
XLA Ops:
  0.0 3.2 %collective-permute-start = (bf16[16,1024]{1,0:T(8,128)(2,1)}, bf16[16,1024]{1,0:T(8,128)(2,1)S(1)}, u32[]{:S(2)}, u32[]{:S(2)}) collective-permute-start(bf16[16,1024]{1,0:T(8,128)(2,1)} %param.5), channel_id=1, source_target_pairs={{0,1},{1,0},{2,3},{3,2},{4,5},{5,4},{6,7},{7,6},{8,9},{9,8},{10,11... | collective-permute-start | bytes 98312 | tf_op jit(solution)/shard_map/out_grads_pair/ppermute | solution.py:43
  6.0 2.9 %collective-permute-start.8 = (bf16[64,896]{1,0:T(8,128)(2,1)}, bf16[64,896]{1,0:T(8,128)(2,1)S(1)}, u32[]{:S(2)}, u32[]{:S(2)}) collective-permute-start(bf16[64,896]{1,0:T(8,128)(2,1)} %refs_0_.1), channel_id=1, source_target_pairs={{0,128},{32,160},{64,192},{96,224},{128,0},{160,32},{192,64},{224,... | collective-permute-start | bytes 344072 | tf_op jit(solution)/shard_map/activations_4/ppermute | solution.py:257
  11.2 6.1 %collective-permute-start.2 = (bf16[64,1024]{1,0:T(8,128)(2,1)S(1)}, bf16[64,1024]{1,0:T(8,128)(2,1)S(1)}, u32[]{:S(2)}, u32[]{:S(2)}) collective-permute-start(bf16[64,1024]{1,0:T(8,128)(2,1)S(1)} %pad_maximum_fusion.8.n0_ref), channel_id=1, source_target_pairs={{0,4},{1,13},{2,6},{3,15},{4,8},{5,1},{6,10},{7,3},{8,12},{9,5},{1... | collective-permute-start | bytes 393224 | tf_op jit(solution)/shard_map/n2/ppermute | solution.py:53
  17.3 2.0 %collective-permute-start.11 = (bf16[64,896]{1,0:T(8,128)(2,1)S(1)}, bf16[64,896]{1,0:T(8,128)(2,1)S(1)}, u32[]{:S(2)}, u32[]{:S(2)}) collective-permute-start(bf16[64,896]{1,0:T(8,128)(2,1)S(1)} %collective-permute-done.5.refs_1_), channel_id=1, source_target_pairs={{0,192},{32,224},{64,0},{96,32},{128,64},{160,96},{192,128},{224,1... | collective-permute-start | bytes 344072 | tf_op jit(solution)/shard_map/activations_6/ppermute | solution.py:257
  21.7 3.2 %collective-permute-done.7.refs_3_ = bf16[64,896]{1,0:T(8,128)(2,1)S(1)} collective-permute-done((bf16[64,896]{1,0:T(8,128)(2,1)S(1)}, bf16[64,896]{1,0:T(8,128)(2,1)S(1)}, u32[]{:S(2)}, u32[]{:S(2)}) %collective-permute-start.7) | collective-permute-done | bytes 114720 | tf_op jit(solution)/shard_map/activations_2/ppermute | solution.py:257
  27.0 3.9 %collective-permute-start.3 = (bf16[128,1024]{1,0:T(8,128)(2,1)S(1)}, bf16[128,1024]{1,0:T(8,128)(2,1)S(1)}, u32[]{:S(2)}, u32[]{:S(2)}) collective-permute-start(bf16[128,1024]{1,0:T(8,128)(2,1)S(1)} %get-tuple-element.35), channel_id=1, source_target_pairs={{0,2},{1,15},{2,4},{3,1},{4,6},{5,3},{6,8},{7,5},{8,10},{9,7},{10,... | collective-permute-start | bytes 786440 | tf_op jit(solution)/shard_map/n13/ppermute | solution.py:48
  32.1 6.7 %rotate.1 = (f32[256,1792]{1,0:T(8,128)S(1)}, f32[256,1792]{1,0:T(8,128)S(1)}) custom-call(bf16[256,896]{1,0:T(8,128)(2,1)S(1)} %get-tuple-element.18.here_rows_ref, bf16[256,896]{1,0:T(8,128)(2,1)S(1)} %collective-permute-done.12.away_rows_ref, bf16[3584,896]{1,0:T(8,128)(2,1)} %here_ref.1, bf16[3584,896]{1,0:T(8,128)(2,1)} %collective-permute-done.13.away_ref), custom_call_target="tpu_custom_call" | custom-call | flops 3288334336 | bytes 12845056 | tf_op jit(solution)/shard_map/rotate/pallas_call | solution.py:226
  42.7 2.0 %collective-permute-start.32 = (bf16[64,1792]{1,0:T(8,128)(2,1)S(1)}, bf16[64,1792]{1,0:T(8,128)(2,1)S(1)}, u32[]{:S(2)}, u32[]{:S(2)}) collective-permute-start(bf16[64,1792]{1,0:T(8,128)(2,1)S(1)} %pad_maximum_fusion.6), channel_id=1, source_target_pairs={{0,2},{1,15},{2,4},{3,1},{4,6},{5,3},{6,8},{7,5},{8,10},{9,7},{10,... | collective-permute-start | bytes 688136 | tf_op jit(solution)/shard_map/step2_0/ppermute | solution.py:48
  44.7 2.2 %collective-permute-start.19 = (bf16[64,1792]{1,0:T(8,128)(2,1)S(1)}, bf16[64,1792]{1,0:T(8,128)(2,1)S(1)}, u32[]{:S(2)}, u32[]{:S(2)}) collective-permute-start(bf16[64,1792]{1,0:T(8,128)(2,1)S(1)} %pad_maximum_fusion.4), channel_id=1, source_target_pairs={{0,2},{1,15},{2,4},{3,1},{4,6},{5,3},{6,8},{7,5},{8,10},{9,7},{10,... | collective-permute-start | bytes 688136 | tf_op jit(solution)/shard_map/step2_1/ppermute | solution.py:48
  48.1 2.8 %collective-permute-start.33 = (bf16[64,1792]{1,0:T(8,128)(2,1)S(1)}, bf16[64,1792]{1,0:T(8,128)(2,1)S(1)}, u32[]{:S(2)}, u32[]{:S(2)}) collective-permute-start(bf16[64,1792]{1,0:T(8,128)(2,1)S(1)} %add_convert_fusion.2), channel_id=1, source_target_pairs={{0,2},{1,15},{2,4},{3,1},{4,6},{5,3},{6,8},{7,5},{8,10},{9,7},{10,... | collective-permute-start | bytes 688136 | tf_op jit(solution)/shard_map/step3_0/ppermute | solution.py:48
  50.9 2.4 %collective-permute-start.20 = (bf16[64,1792]{1,0:T(8,128)(2,1)S(1)}, bf16[64,1792]{1,0:T(8,128)(2,1)S(1)}, u32[]{:S(2)}, u32[]{:S(2)}) collective-permute-start(bf16[64,1792]{1,0:T(8,128)(2,1)S(1)} %add_convert_fusion.4), channel_id=1, source_target_pairs={{0,2},{1,15},{2,4},{3,1},{4,6},{5,3},{6,8},{7,5},{8,10},{9,7},{10,... | collective-permute-start | bytes 688136 | tf_op jit(solution)/shard_map/step3_1/ppermute | solution.py:48
  53.9 3.2 %collective-permute-start.34 = (bf16[64,1792]{1,0:T(8,128)(2,1)S(1)}, bf16[64,1792]{1,0:T(8,128)(2,1)S(1)}, u32[]{:S(2)}, u32[]{:S(2)}) collective-permute-start(bf16[64,1792]{1,0:T(8,128)(2,1)S(1)} %add_convert_fusion.1), channel_id=1, source_target_pairs={{0,2},{1,15},{2,4},{3,1},{4,6},{5,3},{6,8},{7,5},{8,10},{9,7},{10,... | collective-permute-start | bytes 688136 | tf_op jit(solution)/shard_map/step4_0/ppermute | solution.py:48
  57.2 2.4 %collective-permute-start.21 = (bf16[64,1792]{1,0:T(8,128)(2,1)S(1)}, bf16[64,1792]{1,0:T(8,128)(2,1)S(1)}, u32[]{:S(2)}, u32[]{:S(2)}) collective-permute-start(bf16[64,1792]{1,0:T(8,128)(2,1)S(1)} %add_convert_fusion.3), channel_id=1, source_target_pairs={{0,2},{1,15},{2,4},{3,1},{4,6},{5,3},{6,8},{7,5},{8,10},{9,7},{10,... | collective-permute-start | bytes 688136 | tf_op jit(solution)/shard_map/step4_1/ppermute | solution.py:48
  60.1 6.7 %collective-permute-start.35 = (bf16[32,1792]{1,0:T(8,128)(2,1)S(1)}, bf16[32,1792]{1,0:T(8,128)(2,1)S(1)}, u32[]{:S(2)}, u32[]{:S(2)}) collective-permute-start(bf16[32,1792]{1,0:T(8,128)(2,1)S(1)} %slice.97), channel_id=1, source_target_pairs={{0,1},{1,0},{2,3},{3,2},{4,5},{5,4},{6,7},{7,6},{8,9},{9,8},{10,11... | collective-permute-start | bytes 344072 | tf_op jit(solution)/shard_map/other_0/ppermute | solution.py:43
  67.6 2.3 %collective-permute-start.22 = (bf16[32,1792]{1,0:T(8,128)(2,1)S(1)}, bf16[32,1792]{1,0:T(8,128)(2,1)S(1)}, u32[]{:S(2)}, u32[]{:S(2)}) collective-permute-start(bf16[32,1792]{1,0:T(8,128)(2,1)S(1)} %slice.77), channel_id=1, source_target_pairs={{0,1},{1,0},{2,3},{3,2},{4,5},{5,4},{6,7},{7,6},{8,9},{9,8},{10,11... | collective-permute-start | bytes 344072 | tf_op jit(solution)/shard_map/other_1/ppermute | solution.py:43
  70.0 1.8 %collective-permute-start.36 = (bf16[32,1792]{1,0:T(8,128)(2,1)S(1)}, bf16[32,1792]{1,0:T(8,128)(2,1)S(1)}, u32[]{:S(2)}, u32[]{:S(2)}) collective-permute-start(bf16[32,1792]{1,0:T(8,128)(2,1)S(1)} %fusion.1), channel_id=1, source_target_pairs={{0,16},{1,17},{2,18},{3,19},{4,20},{5,21},{6,22},{7,23},{8,24},{9,... | collective-permute-start | bytes 344072 | tf_op jit(solution)/shard_map/across_0/ppermute | solution.py:58
  71.9 1.3 %collective-permute-start.23 = (bf16[32,1792]{1,0:T(8,128)(2,1)S(1)}, bf16[32,1792]{1,0:T(8,128)(2,1)S(1)}, u32[]{:S(2)}, u32[]{:S(2)}) collective-permute-start(bf16[32,1792]{1,0:T(8,128)(2,1)S(1)} %fusion), channel_id=1, source_target_pairs={{0,16},{1,17},{2,18},{3,19},{4,20},{5,21},{6,22},{7,23},{8,24},{9,... | collective-permute-start | bytes 344072 | tf_op jit(solution)/shard_map/across_1/ppermute | solution.py:58
  73.2 3.2 %collective-permute-done.36 = bf16[32,1792]{1,0:T(8,128)(2,1)S(1)} collective-permute-done((bf16[32,1792]{1,0:T(8,128)(2,1)S(1)}, bf16[32,1792]{1,0:T(8,128)(2,1)S(1)}, u32[]{:S(2)}, u32[]{:S(2)}) %collective-permute-start.36) | collective-permute-done | bytes 114720 | tf_op jit(solution)/shard_map/across_0/ppermute | solution.py:58
  76.4 1.3 %collective-permute-start.37 = (bf16[32,1792]{1,0:T(8,128)(2,1)S(1)}, bf16[32,1792]{1,0:T(8,128)(2,1)S(1)}, u32[]{:S(2)}, u32[]{:S(2)}) collective-permute-start(bf16[32,1792]{1,0:T(8,128)(2,1)S(1)} %add_convert_fusion.5.refs_0_), channel_id=1, source_target_pairs={{0,1},{1,0},{2,3},{3,2},{4,5},{5,4},{6,7},{7,6},{8,9},{9,8},{10,11... | collective-permute-start | bytes 344072 | tf_op jit(solution)/shard_map/twin_0/ppermute | solution.py:43
  79.9 1.3 %collective-permute-done.16 = f32[256,512]{1,0:T(8,128)S(1)} collective-permute-done((f32[256,512]{1,0:T(8,128)S(1)}, f32[256,512]{1,0:T(8,128)S(1)}, u32[]{:S(2)}, u32[]{:S(2)}) %collective-permute-start.16) | collective-permute-done | bytes 524320 | tf_op jit(solution)/shard_map/ppermute | solution.py:291
  82.7 2.3 %collective-permute-done.38.refs_2_ = bf16[64,1792]{1,0:T(8,128)(2,1)S(1)} collective-permute-done((bf16[64,1792]{1,0:T(8,128)(2,1)S(1)}, bf16[64,1792]{1,0:T(8,128)(2,1)S(1)}, u32[]{:S(2)}, u32[]{:S(2)}) %collective-permute-start.38) | collective-permute-done | bytes 229408 | tf_op jit(solution)/shard_map/a1_0/ppermute | solution.py:48
  86.0 1.8 %collective-permute-done.25.refs_2_ = bf16[64,1792]{1,0:T(8,128)(2,1)S(1)} collective-permute-done((bf16[64,1792]{1,0:T(8,128)(2,1)S(1)}, bf16[64,1792]{1,0:T(8,128)(2,1)S(1)}, u32[]{:S(2)}, u32[]{:S(2)}) %collective-permute-start.25) | collective-permute-done | bytes 229408 | tf_op jit(solution)/shard_map/a1_1/ppermute | solution.py:48
  88.8 1.5 %collective-permute-done.39.refs_3_ = bf16[64,1792]{1,0:T(8,128)(2,1)S(1)} collective-permute-done((bf16[64,1792]{1,0:T(8,128)(2,1)S(1)}, bf16[64,1792]{1,0:T(8,128)(2,1)S(1)}, u32[]{:S(2)}, u32[]{:S(2)}) %collective-permute-start.39) | collective-permute-done | bytes 229408 | tf_op jit(solution)/shard_map/a2_0/ppermute | solution.py:48
  90.3 1.8 %collective-permute-start.40 = (bf16[64,1792]{1,0:T(8,128)(2,1)S(1)}, bf16[64,1792]{1,0:T(8,128)(2,1)S(1)}, u32[]{:S(2)}, u32[]{:S(2)}) collective-permute-start(bf16[64,1792]{1,0:T(8,128)(2,1)S(1)} %collective-permute-done.39.refs_3_), channel_id=1, source_target_pairs={{0,2},{1,15},{2,4},{3,1},{4,6},{5,3},{6,8},{7,5},{8,10},{9,7},{10,... | collective-permute-start | bytes 688136 | tf_op jit(solution)/shard_map/a3_0/ppermute | solution.py:48
  92.1 2.4 %collective-permute-start.42 = (bf16[128,1792]{1,0:T(8,128)(2,1)S(1)}, bf16[128,1792]{1,0:T(8,128)(2,1)S(1)}, u32[]{:S(2)}, u32[]{:S(2)}) collective-permute-start(bf16[128,1792]{1,0:T(8,128)(2,1)S(1)} %pad_maximum_fusion.1), channel_id=1, source_target_pairs={{0,1},{1,0},{2,3},{3,2},{4,5},{5,4},{6,7},{7,6},{8,9},{9,8},{10,11... | collective-permute-start | bytes 1376264 | tf_op jit(solution)/shard_map/b12_0/ppermute | solution.py:43
  94.6 3.0 %collective-permute-start.27 = (bf16[64,1792]{1,0:T(8,128)(2,1)S(1)}, bf16[64,1792]{1,0:T(8,128)(2,1)S(1)}, u32[]{:S(2)}, u32[]{:S(2)}) collective-permute-start(bf16[64,1792]{1,0:T(8,128)(2,1)S(1)} %collective-permute-done.26.refs_3_), channel_id=1, source_target_pairs={{0,2},{1,15},{2,4},{3,1},{4,6},{5,3},{6,8},{7,5},{8,10},{9,7},{10,... | collective-permute-start | bytes 688136 | tf_op jit(solution)/shard_map/a3_1/ppermute | solution.py:48
  98.4 3.6 %collective-permute-start.29 = (bf16[128,1792]{1,0:T(8,128)(2,1)S(1)}, bf16[128,1792]{1,0:T(8,128)(2,1)S(1)}, u32[]{:S(2)}, u32[]{:S(2)}) collective-permute-start(bf16[128,1792]{1,0:T(8,128)(2,1)S(1)} %pad_maximum_fusion), channel_id=1, source_target_pairs={{0,1},{1,0},{2,3},{3,2},{4,5},{5,4},{6,7},{7,6},{8,9},{9,8},{10,11... | collective-permute-start | bytes 1376264 | tf_op jit(solution)/shard_map/b12_1/ppermute | solution.py:43
  102.0 3.0 %collective-permute-start.28 = (bf16[32,1792]{1,0:T(8,128)(2,1)S(1)}, bf16[32,1792]{1,0:T(8,128)(2,1)S(1)}, u32[]{:S(2)}, u32[]{:S(2)}) collective-permute-start(bf16[32,1792]{1,0:T(8,128)(2,1)S(1)} %slice.93), channel_id=1, source_target_pairs={{0,2},{1,15},{2,4},{3,1},{4,6},{5,3},{6,8},{7,5},{8,10},{9,7},{10,... | collective-permute-start | bytes 344072 | tf_op jit(solution)/shard_map/a4_1/ppermute | solution.py:48
  105.1 2.9 %collective-permute-start.43 = (bf16[96,1792]{1,0:T(8,128)(2,1)S(1)}, bf16[96,1792]{1,0:T(8,128)(2,1)S(1)}, u32[]{:S(2)}, u32[]{:S(2)}) collective-permute-start(bf16[96,1792]{1,0:T(8,128)(2,1)S(1)} %pad_maximum_fusion.3), channel_id=1, source_target_pairs={{0,1},{1,0},{2,3},{3,2},{4,5},{5,4},{6,7},{7,6},{8,9},{9,8},{10,11... | collective-permute-start | bytes 1032200 | tf_op jit(solution)/shard_map/b34_0/ppermute | solution.py:43
  108.0 4.6 %collective-permute-start.30 = (bf16[96,1792]{1,0:T(8,128)(2,1)S(1)}, bf16[96,1792]{1,0:T(8,128)(2,1)S(1)}, u32[]{:S(2)}, u32[]{:S(2)}) collective-permute-start(bf16[96,1792]{1,0:T(8,128)(2,1)S(1)} %pad_maximum_fusion.2), channel_id=1, source_target_pairs={{0,1},{1,0},{2,3},{3,2},{4,5},{5,4},{6,7},{7,6},{8,9},{9,8},{10,11... | collective-permute-start | bytes 1032200 | tf_op jit(solution)/shard_map/b34_1/ppermute | solution.py:43
  112.7 2.2 %finish.2.refs_8_ = f32[256,3584]{1,0:T(8,128)} custom-call(s32[5]{0:T(128)S(1)} %stack.23.place_ref, bf16[256,512]{1,0:T(8,128)(2,1)S(1)} %add_convert_fusion.g_ref, bf16[32,1792]{1,0:T(8,128)(2,1)S(1)} %add_convert_fusion.5.refs_0_, bf16[32,1792]{1,0:T(8,128)(2,1)S(1)} %collective-permute-done.37.refs_1_, ...), custom_call_target="tpu_custom_call" | custom-call | flops 469762048 | bytes 3670016 | tf_op jit(solution)/shard_map/finish/pallas_call | solution.py:114
  114.9 2.2 %finish.3 = f32[256,3584]{1,0:T(8,128)} custom-call(s32[5]{0:T(128)S(1)} %stack.23.place_ref, bf16[256,512]{1,0:T(8,128)(2,1)S(1)} %add_convert_fusion.g_ref, bf16[32,1792]{1,0:T(8,128)(2,1)S(1)} %add_convert_fusion.7.refs_0_, bf16[32,1792]{1,0:T(8,128)(2,1)S(1)} %collective-permute-done.24.refs_1_, ...), custom_call_target="tpu_custom_call", output_to_operand_aliasing={{}: (10, {})} | custom-call | flops 469762048 | bytes 3670016 | tf_op jit(solution)/shard_map/finish/pallas_call | solution.py:114
  (105 shorter events, 24.4 us)
Async XLA Ops:
  4.3 27.8 %collective-permute-start.13 = (bf16[3584,896]{1,0:T(8,128)(2,1)}, bf16[3584,896]{1,0:T(8,128)(2,1)}, u32[]{:S(2)}, u32[]{:S(2)}) collective-permute-start(bf16[3584,896]{1,0:T(8,128)(2,1)} %here_ref.1), channel_id=1, source_target_pairs={{0,1},{1,0},{2,3},{3,2},{4,5},{5,4},{6,7},{7,6},{8,9},{9,8},{10,11... | collective-permute-start | bytes 19267592 | tf_op jit(solution)/shard_map/basis_away/ppermute | solution.py:43
  5.7 5.5 %collective-permute-start.5 = (bf16[64,896]{1,0:T(8,128)(2,1)}, bf16[64,896]{1,0:T(8,128)(2,1)S(1)}, u32[]{:S(2)}, u32[]{:S(2)}) collective-permute-start(bf16[64,896]{1,0:T(8,128)(2,1)} %refs_0_.1), channel_id=1, source_target_pairs={{0,32},{32,0},{64,96},{96,64},{128,160},{160,128},{192,224},{224,1... | collective-permute-start | bytes 344072 | tf_op jit(solution)/shard_map/activations_1/ppermute | solution.py:257
  6.0 11.3 %collective-permute-start.8 = (bf16[64,896]{1,0:T(8,128)(2,1)}, bf16[64,896]{1,0:T(8,128)(2,1)S(1)}, u32[]{:S(2)}, u32[]{:S(2)}) collective-permute-start(bf16[64,896]{1,0:T(8,128)(2,1)} %refs_0_.1), channel_id=1, source_target_pairs={{0,128},{32,160},{64,192},{96,224},{128,0},{160,32},{192,64},{224,... | collective-permute-start | bytes 344072 | tf_op jit(solution)/shard_map/activations_4/ppermute | solution.py:257
  8.9 10.4 %collective-permute-start.10 = (bf16[64,896]{1,0:T(8,128)(2,1)}, bf16[64,896]{1,0:T(8,128)(2,1)S(1)}, u32[]{:S(2)}, u32[]{:S(2)}) collective-permute-start(bf16[64,896]{1,0:T(8,128)(2,1)} %refs_0_.1), channel_id=1, source_target_pairs={{0,192},{32,224},{64,0},{96,32},{128,64},{160,96},{192,128},{224,1... | collective-permute-start | bytes 344072 | tf_op jit(solution)/shard_map/activations_6/ppermute | solution.py:257
  9.7 9.6 %collective-permute-start.6 = (bf16[64,896]{1,0:T(8,128)(2,1)}, bf16[64,896]{1,0:T(8,128)(2,1)S(1)}, u32[]{:S(2)}, u32[]{:S(2)}) collective-permute-start(bf16[64,896]{1,0:T(8,128)(2,1)} %refs_0_.1), channel_id=1, source_target_pairs={{0,64},{32,96},{64,128},{96,160},{128,192},{160,224},{192,0},{224,... | collective-permute-start | bytes 344072 | tf_op jit(solution)/shard_map/activations_2/ppermute | solution.py:257
  11.2 15.4 %collective-permute-start.2 = (bf16[64,1024]{1,0:T(8,128)(2,1)S(1)}, bf16[64,1024]{1,0:T(8,128)(2,1)S(1)}, u32[]{:S(2)}, u32[]{:S(2)}) collective-permute-start(bf16[64,1024]{1,0:T(8,128)(2,1)S(1)} %pad_maximum_fusion.8.n0_ref), channel_id=1, source_target_pairs={{0,4},{1,13},{2,6},{3,15},{4,8},{5,1},{6,10},{7,3},{8,12},{9,5},{1... | collective-permute-start | bytes 393224 | tf_op jit(solution)/shard_map/n2/ppermute | solution.py:53
  19.3 5.6 %collective-permute-start.7 = (bf16[64,896]{1,0:T(8,128)(2,1)S(1)}, bf16[64,896]{1,0:T(8,128)(2,1)S(1)}, u32[]{:S(2)}, u32[]{:S(2)}) collective-permute-start(bf16[64,896]{1,0:T(8,128)(2,1)S(1)} %collective-permute-done.5.refs_1_), channel_id=1, source_target_pairs={{0,64},{32,96},{64,128},{96,160},{128,192},{160,224},{192,0},{224,... | collective-permute-start | bytes 344072 | tf_op jit(solution)/shard_map/activations_2/ppermute | solution.py:257
  19.3 5.6 %collective-permute-start.9 = (bf16[64,896]{1,0:T(8,128)(2,1)S(1)}, bf16[64,896]{1,0:T(8,128)(2,1)S(1)}, u32[]{:S(2)}, u32[]{:S(2)}) collective-permute-start(bf16[64,896]{1,0:T(8,128)(2,1)S(1)} %collective-permute-done.8.refs_4_), channel_id=1, source_target_pairs={{0,32},{32,0},{64,96},{96,64},{128,160},{160,128},{192,224},{224,1... | collective-permute-start | bytes 344072 | tf_op jit(solution)/shard_map/activations_1/ppermute | solution.py:257
  26.5 5.5 %collective-permute-start.12 = (bf16[256,896]{1,0:T(8,128)(2,1)S(1)}, bf16[256,896]{1,0:T(8,128)(2,1)S(1)}, u32[]{:S(2)}, u32[]{:S(2)}) collective-permute-start(bf16[256,896]{1,0:T(8,128)(2,1)S(1)} %get-tuple-element.20), channel_id=1, source_target_pairs={{0,1},{1,0},{2,3},{3,2},{4,5},{5,4},{6,7},{7,6},{8,9},{9,8},{10,11... | collective-permute-start | bytes 1376264 | tf_op jit(solution)/shard_map/x_away/ppermute | solution.py:43
  27.0 12.7 %collective-permute-start.3 = (bf16[128,1024]{1,0:T(8,128)(2,1)S(1)}, bf16[128,1024]{1,0:T(8,128)(2,1)S(1)}, u32[]{:S(2)}, u32[]{:S(2)}) collective-permute-start(bf16[128,1024]{1,0:T(8,128)(2,1)S(1)} %get-tuple-element.35), channel_id=1, source_target_pairs={{0,2},{1,15},{2,4},{3,1},{4,6},{5,3},{6,8},{7,5},{8,10},{9,7},{10,... | collective-permute-start | bytes 786440 | tf_op jit(solution)/shard_map/n13/ppermute | solution.py:48
  30.9 8.8 %collective-permute-start.4 = (bf16[32,1024]{1,0:T(8,128)(2,1)S(1)}, bf16[32,1024]{1,0:T(8,128)(2,1)S(1)}, u32[]{:S(2)}, u32[]{:S(2)}) collective-permute-start(bf16[32,1024]{1,0:T(8,128)(2,1)S(1)} %slice.90), channel_id=1, source_target_pairs={{0,4},{1,13},{2,6},{3,15},{4,8},{5,1},{6,10},{7,3},{8,12},{9,5},{1... | collective-permute-start | bytes 196616 | tf_op jit(solution)/shard_map/n4/ppermute | solution.py:53
  39.8 7.2 %collective-permute-start.14 = (bf16[224,1024]{1,0:T(8,128)(2,1)S(1)}, bf16[224,1024]{1,0:T(8,128)(2,1)S(1)}, u32[]{:S(2)}, u32[]{:S(2)}) collective-permute-start(bf16[224,1024]{1,0:T(8,128)(2,1)S(1)} %constant_dynamic-update-slice_fusion.7.near_ref), channel_id=1, source_target_pairs={{0,1},{1,0},{2,3},{3,2},{4,5},{5,4},{6,7},{7,6},{8,9},{9,8},{10,11... | collective-permute-start | bytes 1376264 | tf_op jit(solution)/shard_map/near_away/ppermute | solution.py:43
  44.7 6.2 %collective-permute-start.19 = (bf16[64,1792]{1,0:T(8,128)(2,1)S(1)}, bf16[64,1792]{1,0:T(8,128)(2,1)S(1)}, u32[]{:S(2)}, u32[]{:S(2)}) collective-permute-start(bf16[64,1792]{1,0:T(8,128)(2,1)S(1)} %pad_maximum_fusion.4), channel_id=1, source_target_pairs={{0,2},{1,15},{2,4},{3,1},{4,6},{5,3},{6,8},{7,5},{8,10},{9,7},{10,... | collective-permute-start | bytes 688136 | tf_op jit(solution)/shard_map/step2_1/ppermute | solution.py:48
  48.1 5.8 %collective-permute-start.33 = (bf16[64,1792]{1,0:T(8,128)(2,1)S(1)}, bf16[64,1792]{1,0:T(8,128)(2,1)S(1)}, u32[]{:S(2)}, u32[]{:S(2)}) collective-permute-start(bf16[64,1792]{1,0:T(8,128)(2,1)S(1)} %add_convert_fusion.2), channel_id=1, source_target_pairs={{0,2},{1,15},{2,4},{3,1},{4,6},{5,3},{6,8},{7,5},{8,10},{9,7},{10,... | collective-permute-start | bytes 688136 | tf_op jit(solution)/shard_map/step3_0/ppermute | solution.py:48
  50.9 6.2 %collective-permute-start.20 = (bf16[64,1792]{1,0:T(8,128)(2,1)S(1)}, bf16[64,1792]{1,0:T(8,128)(2,1)S(1)}, u32[]{:S(2)}, u32[]{:S(2)}) collective-permute-start(bf16[64,1792]{1,0:T(8,128)(2,1)S(1)} %add_convert_fusion.4), channel_id=1, source_target_pairs={{0,2},{1,15},{2,4},{3,1},{4,6},{5,3},{6,8},{7,5},{8,10},{9,7},{10,... | collective-permute-start | bytes 688136 | tf_op jit(solution)/shard_map/step3_1/ppermute | solution.py:48
  53.4 13.5 %collective-permute-start.15 = (f32[256,512]{1,0:T(8,128)S(1)}, f32[256,512]{1,0:T(8,128)S(1)}, u32[]{:S(2)}, u32[]{:S(2)}) collective-permute-start(f32[256,512]{1,0:T(8,128)S(1)} %rotate_grads.1), channel_id=1, source_target_pairs={{0,64},{32,96},{64,0},{96,32},{128,192},{160,224},{192,128},{224,1... | collective-permute-start | bytes 1572872 | tf_op jit(solution)/shard_map/ppermute | solution.py:284
  53.9 6.2 %collective-permute-start.34 = (bf16[64,1792]{1,0:T(8,128)(2,1)S(1)}, bf16[64,1792]{1,0:T(8,128)(2,1)S(1)}, u32[]{:S(2)}, u32[]{:S(2)}) collective-permute-start(bf16[64,1792]{1,0:T(8,128)(2,1)S(1)} %add_convert_fusion.1), channel_id=1, source_target_pairs={{0,2},{1,15},{2,4},{3,1},{4,6},{5,3},{6,8},{7,5},{8,10},{9,7},{10,... | collective-permute-start | bytes 688136 | tf_op jit(solution)/shard_map/step4_0/ppermute | solution.py:48
  57.2 10.4 %collective-permute-start.21 = (bf16[64,1792]{1,0:T(8,128)(2,1)S(1)}, bf16[64,1792]{1,0:T(8,128)(2,1)S(1)}, u32[]{:S(2)}, u32[]{:S(2)}) collective-permute-start(bf16[64,1792]{1,0:T(8,128)(2,1)S(1)} %add_convert_fusion.3), channel_id=1, source_target_pairs={{0,2},{1,15},{2,4},{3,1},{4,6},{5,3},{6,8},{7,5},{8,10},{9,7},{10,... | collective-permute-start | bytes 688136 | tf_op jit(solution)/shard_map/step4_1/ppermute | solution.py:48
  60.1 9.8 %collective-permute-start.35 = (bf16[32,1792]{1,0:T(8,128)(2,1)S(1)}, bf16[32,1792]{1,0:T(8,128)(2,1)S(1)}, u32[]{:S(2)}, u32[]{:S(2)}) collective-permute-start(bf16[32,1792]{1,0:T(8,128)(2,1)S(1)} %slice.97), channel_id=1, source_target_pairs={{0,1},{1,0},{2,3},{3,2},{4,5},{5,4},{6,7},{7,6},{8,9},{9,8},{10,11... | collective-permute-start | bytes 344072 | tf_op jit(solution)/shard_map/other_0/ppermute | solution.py:43
  66.9 14.4 %collective-permute-start.16 = (f32[256,512]{1,0:T(8,128)S(1)}, f32[256,512]{1,0:T(8,128)S(1)}, u32[]{:S(2)}, u32[]{:S(2)}) collective-permute-start(f32[256,512]{1,0:T(8,128)S(1)} %add.61), channel_id=1, source_target_pairs={{0,128},{32,160},{64,192},{96,224},{128,0},{160,32},{192,64},{224,... | collective-permute-start | bytes 1572872 | tf_op jit(solution)/shard_map/ppermute | solution.py:291
  70.0 6.4 %collective-permute-start.36 = (bf16[32,1792]{1,0:T(8,128)(2,1)S(1)}, bf16[32,1792]{1,0:T(8,128)(2,1)S(1)}, u32[]{:S(2)}, u32[]{:S(2)}) collective-permute-start(bf16[32,1792]{1,0:T(8,128)(2,1)S(1)} %fusion.1), channel_id=1, source_target_pairs={{0,16},{1,17},{2,18},{3,19},{4,20},{5,21},{6,22},{7,23},{8,24},{9,... | collective-permute-start | bytes 344072 | tf_op jit(solution)/shard_map/across_0/ppermute | solution.py:58
  71.9 6.9 %collective-permute-start.23 = (bf16[32,1792]{1,0:T(8,128)(2,1)S(1)}, bf16[32,1792]{1,0:T(8,128)(2,1)S(1)}, u32[]{:S(2)}, u32[]{:S(2)}) collective-permute-start(bf16[32,1792]{1,0:T(8,128)(2,1)S(1)} %fusion), channel_id=1, source_target_pairs={{0,16},{1,17},{2,18},{3,19},{4,20},{5,21},{6,22},{7,23},{8,24},{9,... | collective-permute-start | bytes 344072 | tf_op jit(solution)/shard_map/across_1/ppermute | solution.py:58
  81.3 16.2 %collective-permute-start.17 = (f32[256,512]{1,0:T(8,128)S(1)}, f32[256,512]{1,0:T(8,128)S(1)}, u32[]{:S(2)}, u32[]{:S(2)}) collective-permute-start(f32[256,512]{1,0:T(8,128)S(1)} %add.62), channel_id=1, source_target_pairs={{0,32},{32,0},{64,96},{96,64},{128,160},{160,128},{192,224},{224,1... | collective-permute-start | bytes 1572872 | tf_op jit(solution)/shard_map/ppermute | solution.py:299
  87.9 6.7 %collective-permute-start.26 = (bf16[64,1792]{1,0:T(8,128)(2,1)S(1)}, bf16[64,1792]{1,0:T(8,128)(2,1)S(1)}, u32[]{:S(2)}, u32[]{:S(2)}) collective-permute-start(bf16[64,1792]{1,0:T(8,128)(2,1)S(1)} %collective-permute-done.25.refs_2_), channel_id=1, source_target_pairs={{0,2},{1,15},{2,4},{3,1},{4,6},{5,3},{6,8},{7,5},{8,10},{9,7},{10,... | collective-permute-start | bytes 688136 | tf_op jit(solution)/shard_map/a2_1/ppermute | solution.py:48
  90.3 7.2 %collective-permute-start.40 = (bf16[64,1792]{1,0:T(8,128)(2,1)S(1)}, bf16[64,1792]{1,0:T(8,128)(2,1)S(1)}, u32[]{:S(2)}, u32[]{:S(2)}) collective-permute-start(bf16[64,1792]{1,0:T(8,128)(2,1)S(1)} %collective-permute-done.39.refs_3_), channel_id=1, source_target_pairs={{0,2},{1,15},{2,4},{3,1},{4,6},{5,3},{6,8},{7,5},{8,10},{9,7},{10,... | collective-permute-start | bytes 688136 | tf_op jit(solution)/shard_map/a3_0/ppermute | solution.py:48
  92.1 20.5 %collective-permute-start.42 = (bf16[128,1792]{1,0:T(8,128)(2,1)S(1)}, bf16[128,1792]{1,0:T(8,128)(2,1)S(1)}, u32[]{:S(2)}, u32[]{:S(2)}) collective-permute-start(bf16[128,1792]{1,0:T(8,128)(2,1)S(1)} %pad_maximum_fusion.1), channel_id=1, source_target_pairs={{0,1},{1,0},{2,3},{3,2},{4,5},{5,4},{6,7},{7,6},{8,9},{9,8},{10,11... | collective-permute-start | bytes 1376264 | tf_op jit(solution)/shard_map/b12_0/ppermute | solution.py:43
  94.6 7.4 %collective-permute-start.27 = (bf16[64,1792]{1,0:T(8,128)(2,1)S(1)}, bf16[64,1792]{1,0:T(8,128)(2,1)S(1)}, u32[]{:S(2)}, u32[]{:S(2)}) collective-permute-start(bf16[64,1792]{1,0:T(8,128)(2,1)S(1)} %collective-permute-done.26.refs_3_), channel_id=1, source_target_pairs={{0,2},{1,15},{2,4},{3,1},{4,6},{5,3},{6,8},{7,5},{8,10},{9,7},{10,... | collective-permute-start | bytes 688136 | tf_op jit(solution)/shard_map/a3_1/ppermute | solution.py:48
  97.6 7.4 %collective-permute-start.41 = (bf16[32,1792]{1,0:T(8,128)(2,1)S(1)}, bf16[32,1792]{1,0:T(8,128)(2,1)S(1)}, u32[]{:S(2)}, u32[]{:S(2)}) collective-permute-start(bf16[32,1792]{1,0:T(8,128)(2,1)S(1)} %slice.98), channel_id=1, source_target_pairs={{0,2},{1,15},{2,4},{3,1},{4,6},{5,3},{6,8},{7,5},{8,10},{9,7},{10,... | collective-permute-start | bytes 344072 | tf_op jit(solution)/shard_map/a4_0/ppermute | solution.py:48
  98.4 16.5 %collective-permute-start.29 = (bf16[128,1792]{1,0:T(8,128)(2,1)S(1)}, bf16[128,1792]{1,0:T(8,128)(2,1)S(1)}, u32[]{:S(2)}, u32[]{:S(2)}) collective-permute-start(bf16[128,1792]{1,0:T(8,128)(2,1)S(1)} %pad_maximum_fusion), channel_id=1, source_target_pairs={{0,1},{1,0},{2,3},{3,2},{4,5},{5,4},{6,7},{7,6},{8,9},{9,8},{10,11... | collective-permute-start | bytes 1376264 | tf_op jit(solution)/shard_map/b12_1/ppermute | solution.py:43
  102.0 6.0 %collective-permute-start.28 = (bf16[32,1792]{1,0:T(8,128)(2,1)S(1)}, bf16[32,1792]{1,0:T(8,128)(2,1)S(1)}, u32[]{:S(2)}, u32[]{:S(2)}) collective-permute-start(bf16[32,1792]{1,0:T(8,128)(2,1)S(1)} %slice.93), channel_id=1, source_target_pairs={{0,2},{1,15},{2,4},{3,1},{4,6},{5,3},{6,8},{7,5},{8,10},{9,7},{10,... | collective-permute-start | bytes 344072 | tf_op jit(solution)/shard_map/a4_1/ppermute | solution.py:48
  105.1 7.6 %collective-permute-start.43 = (bf16[96,1792]{1,0:T(8,128)(2,1)S(1)}, bf16[96,1792]{1,0:T(8,128)(2,1)S(1)}, u32[]{:S(2)}, u32[]{:S(2)}) collective-permute-start(bf16[96,1792]{1,0:T(8,128)(2,1)S(1)} %pad_maximum_fusion.3), channel_id=1, source_target_pairs={{0,1},{1,0},{2,3},{3,2},{4,5},{5,4},{6,7},{7,6},{8,9},{9,8},{10,11... | collective-permute-start | bytes 1032200 | tf_op jit(solution)/shard_map/b34_0/ppermute | solution.py:43
  108.0 6.9 %collective-permute-start.30 = (bf16[96,1792]{1,0:T(8,128)(2,1)S(1)}, bf16[96,1792]{1,0:T(8,128)(2,1)S(1)}, u32[]{:S(2)}, u32[]{:S(2)}) collective-permute-start(bf16[96,1792]{1,0:T(8,128)(2,1)S(1)} %pad_maximum_fusion.2), channel_id=1, source_target_pairs={{0,1},{1,0},{2,3},{3,2},{4,5},{5,4},{6,7},{7,6},{8,9},{9,8},{10,11... | collective-permute-start | bytes 1032200 | tf_op jit(solution)/shard_map/b34_1/ppermute | solution.py:43
  (14 other events, 60.8 us)

commit v2 on v1

--- a/solution.py
+++ b/solution.py
@@ -79,7 +79,7 @@
 
 
 LAYOUT = [[(0, 0)], [(0, 1)], block(-1), block(-2), block(-3), [(4, 0)]]
-LAYOUT = LAYOUT + [mirrored(block(-1) + block(-2)), mirrored(block(-3) + [(4, 0)])]
+LAYOUT = LAYOUT + [mirrored(block(-1) + block(-2) + block(-3) + [(4, 0)])]
 
 
 def finish_kernel(width, first, aliased, place_ref, g_ref, *refs):
@@ -299,14 +299,13 @@
     g_away = lax.ppermute(g, "dp", XLO)
     a1[0] = after(a1[0], g)
     a2 = [ahead(a1[s], f"a2_{s}") for s in streams]
-    b12 = [swap(cat(a1[s], a2[s]), f"b12_{s}") for s in streams]
     a3 = [ahead(a2[s], f"a3_{s}") for s in streams]
     g = (g + g_away).astype(BF)
     a4 = [ahead(after(a3[s][:32], g), f"a4_{s}") for s in streams]
-    b34 = [swap(cat(a3[s], a4[s]), f"b34_{s}") for s in streams]
+    others = [swap(cat(a1[s], a2[s], a3[s], a4[s]), f"others_{s}") for s in streams]
     out = None
     for s in streams:
-        parts = [x[s] for x in (own, twin, a1, a2, a3, a4, b12, b34)]
+        parts = [x[s] for x in (own, twin, a1, a2, a3, a4, others)]
         out = finish(place, g, parts, width, s * width, whole, out)
     return out
 

time: 118 us -> 118 us (level)
  starting transfers between devices: 82.5 us -> 81.1 us
  waiting for transfers between devices: 17.7 us -> 19.1 us
    ppermute x12 -> x10, starting transfers between devices: 29.7 us -> 27.7 us  [swap(): return lax.ppermute(x, 'mp', CORE)]
    ppermute x17, waiting for transfers between devices: 7.42 us -> 8.84 us  [ahead(): return lax.ppermute(x, 'mp', AHEAD)]
  transfers between devices with their start and end apart: 44 -> 42, of which waited for: 12 -> 14; matrix products, arithmetic and copies ran while one was open for 2% -> 2% of each run, Pallas kernels for 9% -> 9%
where the time goes in v2:
time: 118 us; the launch traced here: 117 us
  starting transfers between devices  81.1 us (69%)
  waiting for transfers between devices  19.1 us (16%)
  Pallas kernels  13 us (11%)
  local copies, waits for them, and re-layouts  1.88 us (2%)
  other arithmetic  1.83 us (2%)
    ppermute x17, starting transfers between devices, ahead(): return lax.ppermute(x, 'mp', AHEAD)  32.1 us
    ppermute x10, starting transfers between devices, swap(): return lax.ppermute(x, 'mp', CORE)  27.7 us
    ppermute x17, waiting for transfers between devices, ahead(): return lax.ppermute(x, 'mp', AHEAD)  8.84 us
    ppermute x7, starting transfers between devices, shift(): return lax.ppermute(x, 'dp', dp_perm(lambda y, l: (y + b // 2, l + b % 2)))  7.91 us
    ppermute x2, starting transfers between devices, ahead2(): return lax.ppermute(x, 'mp', AHEAD2)  7.27 us
    pallas_call x1, Pallas kernels, rotate(): pl.pallas_call(functools.partial(rotate_kernel, cuts), out_shape=[jax.Sha...  6.7 us
    pallas_call x2, Pallas kernels, finish(): pl.pallas_call(functools.partial(finish_kernel, width, first, int(aliased...  4.43 us
    ppermute x7, waiting for transfers between devices, shift(): return lax.ppermute(x, 'dp', dp_perm(lambda y, l: (y + b // 2, l + b % 2)))  4.3 us
  transfers between devices with their start and end apart: 42, of which 14 were waited for; matrix products, arithmetic and copies ran while one was open for 2% of the time, Pallas kernels for 9%

profile of v2, /device:TPU:1, one launch (start us, length us, event | category | flops | bytes accessed | tf_op | source)
XLA Modules:
  0.0 117.3 jit_solution(16394863358626856959)
XLA Ops:
  0.0 3.2 %collective-permute-start = (bf16[16,1024]{1,0:T(8,128)(2,1)}, bf16[16,1024]{1,0:T(8,128)(2,1)S(1)}, u32[]{:S(2)}, u32[]{:S(2)}) collective-permute-start(bf16[16,1024]{1,0:T(8,128)(2,1)} %param.5), channel_id=1, source_target_pairs={{0,1},{1,0},{2,3},{3,2},{4,5},{5,4},{6,7},{7,6},{8,9},{9,8},{10,11... | collective-permute-start | bytes 98312 | tf_op jit(solution)/shard_map/out_grads_pair/ppermute | solution.py:43
  6.0 2.9 %collective-permute-start.8 = (bf16[64,896]{1,0:T(8,128)(2,1)}, bf16[64,896]{1,0:T(8,128)(2,1)S(1)}, u32[]{:S(2)}, u32[]{:S(2)}) collective-permute-start(bf16[64,896]{1,0:T(8,128)(2,1)} %refs_0_.1), channel_id=1, source_target_pairs={{0,128},{32,160},{64,192},{96,224},{128,0},{160,32},{192,64},{224,... | collective-permute-start | bytes 344072 | tf_op jit(solution)/shard_map/activations_4/ppermute | solution.py:257
  11.2 6.1 %collective-permute-start.2 = (bf16[64,1024]{1,0:T(8,128)(2,1)S(1)}, bf16[64,1024]{1,0:T(8,128)(2,1)S(1)}, u32[]{:S(2)}, u32[]{:S(2)}) collective-permute-start(bf16[64,1024]{1,0:T(8,128)(2,1)S(1)} %pad_maximum_fusion.6.n0_ref), channel_id=1, source_target_pairs={{0,4},{1,13},{2,6},{3,15},{4,8},{5,1},{6,10},{7,3},{8,12},{9,5},{1... | collective-permute-start | bytes 393224 | tf_op jit(solution)/shard_map/n2/ppermute | solution.py:53
  17.3 2.0 %collective-permute-start.11 = (bf16[64,896]{1,0:T(8,128)(2,1)S(1)}, bf16[64,896]{1,0:T(8,128)(2,1)S(1)}, u32[]{:S(2)}, u32[]{:S(2)}) collective-permute-start(bf16[64,896]{1,0:T(8,128)(2,1)S(1)} %collective-permute-done.5.refs_1_), channel_id=1, source_target_pairs={{0,192},{32,224},{64,0},{96,32},{128,64},{160,96},{192,128},{224,1... | collective-permute-start | bytes 344072 | tf_op jit(solution)/shard_map/activations_6/ppermute | solution.py:257
  19.3 1.3 %collective-permute-start.9 = (bf16[64,896]{1,0:T(8,128)(2,1)S(1)}, bf16[64,896]{1,0:T(8,128)(2,1)S(1)}, u32[]{:S(2)}, u32[]{:S(2)}) collective-permute-start(bf16[64,896]{1,0:T(8,128)(2,1)S(1)} %collective-permute-done.8.refs_4_), channel_id=1, source_target_pairs={{0,32},{32,0},{64,96},{96,64},{128,160},{160,128},{192,224},{224,1... | collective-permute-start | bytes 344072 | tf_op jit(solution)/shard_map/activations_1/ppermute | solution.py:257
  21.7 3.2 %collective-permute-done.7.refs_3_ = bf16[64,896]{1,0:T(8,128)(2,1)S(1)} collective-permute-done((bf16[64,896]{1,0:T(8,128)(2,1)S(1)}, bf16[64,896]{1,0:T(8,128)(2,1)S(1)}, u32[]{:S(2)}, u32[]{:S(2)}) %collective-permute-start.7) | collective-permute-done | bytes 114720 | tf_op jit(solution)/shard_map/activations_2/ppermute | solution.py:257
  27.0 3.9 %collective-permute-start.3 = (bf16[128,1024]{1,0:T(8,128)(2,1)S(1)}, bf16[128,1024]{1,0:T(8,128)(2,1)S(1)}, u32[]{:S(2)}, u32[]{:S(2)}) collective-permute-start(bf16[128,1024]{1,0:T(8,128)(2,1)S(1)} %get-tuple-element.35), channel_id=1, source_target_pairs={{0,2},{1,15},{2,4},{3,1},{4,6},{5,3},{6,8},{7,5},{8,10},{9,7},{10,... | collective-permute-start | bytes 786440 | tf_op jit(solution)/shard_map/n13/ppermute | solution.py:48
  32.1 6.7 %rotate.1 = (f32[256,1792]{1,0:T(8,128)S(1)}, f32[256,1792]{1,0:T(8,128)S(1)}) custom-call(bf16[256,896]{1,0:T(8,128)(2,1)S(1)} %get-tuple-element.18.here_rows_ref, bf16[256,896]{1,0:T(8,128)(2,1)S(1)} %collective-permute-done.12.away_rows_ref, bf16[3584,896]{1,0:T(8,128)(2,1)} %here_ref.1, bf16[3584,896]{1,0:T(8,128)(2,1)} %collective-permute-done.13.away_ref), custom_call_target="tpu_custom_call" | custom-call | flops 3288334336 | bytes 12845056 | tf_op jit(solution)/shard_map/rotate/pallas_call | solution.py:226
  42.7 2.0 %collective-permute-start.31 = (bf16[64,1792]{1,0:T(8,128)(2,1)S(1)}, bf16[64,1792]{1,0:T(8,128)(2,1)S(1)}, u32[]{:S(2)}, u32[]{:S(2)}) collective-permute-start(bf16[64,1792]{1,0:T(8,128)(2,1)S(1)} %pad_maximum_fusion.4), channel_id=1, source_target_pairs={{0,2},{1,15},{2,4},{3,1},{4,6},{5,3},{6,8},{7,5},{8,10},{9,7},{10,... | collective-permute-start | bytes 688136 | tf_op jit(solution)/shard_map/step2_0/ppermute | solution.py:48
  44.7 2.2 %collective-permute-start.19 = (bf16[64,1792]{1,0:T(8,128)(2,1)S(1)}, bf16[64,1792]{1,0:T(8,128)(2,1)S(1)}, u32[]{:S(2)}, u32[]{:S(2)}) collective-permute-start(bf16[64,1792]{1,0:T(8,128)(2,1)S(1)} %pad_maximum_fusion.2), channel_id=1, source_target_pairs={{0,2},{1,15},{2,4},{3,1},{4,6},{5,3},{6,8},{7,5},{8,10},{9,7},{10,... | collective-permute-start | bytes 688136 | tf_op jit(solution)/shard_map/step2_1/ppermute | solution.py:48
  48.1 2.8 %collective-permute-start.32 = (bf16[64,1792]{1,0:T(8,128)(2,1)S(1)}, bf16[64,1792]{1,0:T(8,128)(2,1)S(1)}, u32[]{:S(2)}, u32[]{:S(2)}) collective-permute-start(bf16[64,1792]{1,0:T(8,128)(2,1)S(1)} %add_convert_fusion.2), channel_id=1, source_target_pairs={{0,2},{1,15},{2,4},{3,1},{4,6},{5,3},{6,8},{7,5},{8,10},{9,7},{10,... | collective-permute-start | bytes 688136 | tf_op jit(solution)/shard_map/step3_0/ppermute | solution.py:48
  50.9 2.4 %collective-permute-start.20 = (bf16[64,1792]{1,0:T(8,128)(2,1)S(1)}, bf16[64,1792]{1,0:T(8,128)(2,1)S(1)}, u32[]{:S(2)}, u32[]{:S(2)}) collective-permute-start(bf16[64,1792]{1,0:T(8,128)(2,1)S(1)} %add_convert_fusion.4), channel_id=1, source_target_pairs={{0,2},{1,15},{2,4},{3,1},{4,6},{5,3},{6,8},{7,5},{8,10},{9,7},{10,... | collective-permute-start | bytes 688136 | tf_op jit(solution)/shard_map/step3_1/ppermute | solution.py:48
  53.9 3.2 %collective-permute-start.33 = (bf16[64,1792]{1,0:T(8,128)(2,1)S(1)}, bf16[64,1792]{1,0:T(8,128)(2,1)S(1)}, u32[]{:S(2)}, u32[]{:S(2)}) collective-permute-start(bf16[64,1792]{1,0:T(8,128)(2,1)S(1)} %add_convert_fusion.1), channel_id=1, source_target_pairs={{0,2},{1,15},{2,4},{3,1},{4,6},{5,3},{6,8},{7,5},{8,10},{9,7},{10,... | collective-permute-start | bytes 688136 | tf_op jit(solution)/shard_map/step4_0/ppermute | solution.py:48
  57.2 2.4 %collective-permute-start.21 = (bf16[64,1792]{1,0:T(8,128)(2,1)S(1)}, bf16[64,1792]{1,0:T(8,128)(2,1)S(1)}, u32[]{:S(2)}, u32[]{:S(2)}) collective-permute-start(bf16[64,1792]{1,0:T(8,128)(2,1)S(1)} %add_convert_fusion.3), channel_id=1, source_target_pairs={{0,2},{1,15},{2,4},{3,1},{4,6},{5,3},{6,8},{7,5},{8,10},{9,7},{10,... | collective-permute-start | bytes 688136 | tf_op jit(solution)/shard_map/step4_1/ppermute | solution.py:48
  60.1 6.7 %collective-permute-start.34 = (bf16[32,1792]{1,0:T(8,128)(2,1)S(1)}, bf16[32,1792]{1,0:T(8,128)(2,1)S(1)}, u32[]{:S(2)}, u32[]{:S(2)}) collective-permute-start(bf16[32,1792]{1,0:T(8,128)(2,1)S(1)} %slice.97), channel_id=1, source_target_pairs={{0,1},{1,0},{2,3},{3,2},{4,5},{5,4},{6,7},{7,6},{8,9},{9,8},{10,11... | collective-permute-start | bytes 344072 | tf_op jit(solution)/shard_map/other_0/ppermute | solution.py:43
  67.6 2.3 %collective-permute-start.22 = (bf16[32,1792]{1,0:T(8,128)(2,1)S(1)}, bf16[32,1792]{1,0:T(8,128)(2,1)S(1)}, u32[]{:S(2)}, u32[]{:S(2)}) collective-permute-start(bf16[32,1792]{1,0:T(8,128)(2,1)S(1)} %slice.77), channel_id=1, source_target_pairs={{0,1},{1,0},{2,3},{3,2},{4,5},{5,4},{6,7},{7,6},{8,9},{9,8},{10,11... | collective-permute-start | bytes 344072 | tf_op jit(solution)/shard_map/other_1/ppermute | solution.py:43
  70.0 1.8 %collective-permute-start.35 = (bf16[32,1792]{1,0:T(8,128)(2,1)S(1)}, bf16[32,1792]{1,0:T(8,128)(2,1)S(1)}, u32[]{:S(2)}, u32[]{:S(2)}) collective-permute-start(bf16[32,1792]{1,0:T(8,128)(2,1)S(1)} %fusion.1), channel_id=1, source_target_pairs={{0,16},{1,17},{2,18},{3,19},{4,20},{5,21},{6,22},{7,23},{8,24},{9,... | collective-permute-start | bytes 344072 | tf_op jit(solution)/shard_map/across_0/ppermute | solution.py:58
  71.9 1.3 %collective-permute-start.23 = (bf16[32,1792]{1,0:T(8,128)(2,1)S(1)}, bf16[32,1792]{1,0:T(8,128)(2,1)S(1)}, u32[]{:S(2)}, u32[]{:S(2)}) collective-permute-start(bf16[32,1792]{1,0:T(8,128)(2,1)S(1)} %fusion), channel_id=1, source_target_pairs={{0,16},{1,17},{2,18},{3,19},{4,20},{5,21},{6,22},{7,23},{8,24},{9,... | collective-permute-start | bytes 344072 | tf_op jit(solution)/shard_map/across_1/ppermute | solution.py:58
  73.2 3.2 %collective-permute-done.35 = bf16[32,1792]{1,0:T(8,128)(2,1)S(1)} collective-permute-done((bf16[32,1792]{1,0:T(8,128)(2,1)S(1)}, bf16[32,1792]{1,0:T(8,128)(2,1)S(1)}, u32[]{:S(2)}, u32[]{:S(2)}) %collective-permute-start.35) | collective-permute-done | bytes 114720 | tf_op jit(solution)/shard_map/across_0/ppermute | solution.py:58
  76.4 1.3 %collective-permute-start.36 = (bf16[32,1792]{1,0:T(8,128)(2,1)S(1)}, bf16[32,1792]{1,0:T(8,128)(2,1)S(1)}, u32[]{:S(2)}, u32[]{:S(2)}) collective-permute-start(bf16[32,1792]{1,0:T(8,128)(2,1)S(1)} %add_convert_fusion.5.refs_0_), channel_id=1, source_target_pairs={{0,1},{1,0},{2,3},{3,2},{4,5},{5,4},{6,7},{7,6},{8,9},{9,8},{10,11... | collective-permute-start | bytes 344072 | tf_op jit(solution)/shard_map/twin_0/ppermute | solution.py:43
  79.9 1.3 %collective-permute-done.16 = f32[256,512]{1,0:T(8,128)S(1)} collective-permute-done((f32[256,512]{1,0:T(8,128)S(1)}, f32[256,512]{1,0:T(8,128)S(1)}, u32[]{:S(2)}, u32[]{:S(2)}) %collective-permute-start.16) | collective-permute-done | bytes 524320 | tf_op jit(solution)/shard_map/ppermute | solution.py:291
  82.7 2.3 %collective-permute-done.37.refs_2_ = bf16[64,1792]{1,0:T(8,128)(2,1)S(1)} collective-permute-done((bf16[64,1792]{1,0:T(8,128)(2,1)S(1)}, bf16[64,1792]{1,0:T(8,128)(2,1)S(1)}, u32[]{:S(2)}, u32[]{:S(2)}) %collective-permute-start.37) | collective-permute-done | bytes 229408 | tf_op jit(solution)/shard_map/a1_0/ppermute | solution.py:48
  86.0 1.8 %collective-permute-done.25.refs_2_ = bf16[64,1792]{1,0:T(8,128)(2,1)S(1)} collective-permute-done((bf16[64,1792]{1,0:T(8,128)(2,1)S(1)}, bf16[64,1792]{1,0:T(8,128)(2,1)S(1)}, u32[]{:S(2)}, u32[]{:S(2)}) %collective-permute-start.25) | collective-permute-done | bytes 229408 | tf_op jit(solution)/shard_map/a1_1/ppermute | solution.py:48
  88.8 1.5 %collective-permute-done.38.refs_3_ = bf16[64,1792]{1,0:T(8,128)(2,1)S(1)} collective-permute-done((bf16[64,1792]{1,0:T(8,128)(2,1)S(1)}, bf16[64,1792]{1,0:T(8,128)(2,1)S(1)}, u32[]{:S(2)}, u32[]{:S(2)}) %collective-permute-start.38) | collective-permute-done | bytes 229408 | tf_op jit(solution)/shard_map/a2_0/ppermute | solution.py:48
  90.3 1.8 %collective-permute-start.39 = (bf16[64,1792]{1,0:T(8,128)(2,1)S(1)}, bf16[64,1792]{1,0:T(8,128)(2,1)S(1)}, u32[]{:S(2)}, u32[]{:S(2)}) collective-permute-start(bf16[64,1792]{1,0:T(8,128)(2,1)S(1)} %collective-permute-done.38.refs_3_), channel_id=1, source_target_pairs={{0,2},{1,15},{2,4},{3,1},{4,6},{5,3},{6,8},{7,5},{8,10},{9,7},{10,... | collective-permute-start | bytes 688136 | tf_op jit(solution)/shard_map/a3_0/ppermute | solution.py:48
  93.0 1.8 %collective-permute-start.27 = (bf16[64,1792]{1,0:T(8,128)(2,1)S(1)}, bf16[64,1792]{1,0:T(8,128)(2,1)S(1)}, u32[]{:S(2)}, u32[]{:S(2)}) collective-permute-start(bf16[64,1792]{1,0:T(8,128)(2,1)S(1)} %collective-permute-done.26.refs_3_), channel_id=1, source_target_pairs={{0,2},{1,15},{2,4},{3,1},{4,6},{5,3},{6,8},{7,5},{8,10},{9,7},{10,... | collective-permute-start | bytes 688136 | tf_op jit(solution)/shard_map/a3_1/ppermute | solution.py:48
  95.5 2.9 %collective-permute-start.40 = (bf16[32,1792]{1,0:T(8,128)(2,1)S(1)}, bf16[32,1792]{1,0:T(8,128)(2,1)S(1)}, u32[]{:S(2)}, u32[]{:S(2)}) collective-permute-start(bf16[32,1792]{1,0:T(8,128)(2,1)S(1)} %slice.98), channel_id=1, source_target_pairs={{0,2},{1,15},{2,4},{3,1},{4,6},{5,3},{6,8},{7,5},{8,10},{9,7},{10,... | collective-permute-start | bytes 344072 | tf_op jit(solution)/shard_map/a4_0/ppermute | solution.py:48
  98.4 2.6 %collective-permute-start.28 = (bf16[32,1792]{1,0:T(8,128)(2,1)S(1)}, bf16[32,1792]{1,0:T(8,128)(2,1)S(1)}, u32[]{:S(2)}, u32[]{:S(2)}) collective-permute-start(bf16[32,1792]{1,0:T(8,128)(2,1)S(1)} %slice.93), channel_id=1, source_target_pairs={{0,2},{1,15},{2,4},{3,1},{4,6},{5,3},{6,8},{7,5},{8,10},{9,7},{10,... | collective-permute-start | bytes 344072 | tf_op jit(solution)/shard_map/a4_1/ppermute | solution.py:48
  101.1 6.9 %collective-permute-start.41 = (bf16[224,1792]{1,0:T(8,128)(2,1)S(1)}, bf16[224,1792]{1,0:T(8,128)(2,1)S(1)}, u32[]{:S(2)}, u32[]{:S(2)}) collective-permute-start(bf16[224,1792]{1,0:T(8,128)(2,1)S(1)} %pad_maximum_fusion.1), channel_id=1, source_target_pairs={{0,1},{1,0},{2,3},{3,2},{4,5},{5,4},{6,7},{7,6},{8,9},{9,8},{10,11... | collective-permute-start | bytes 2408456 | tf_op jit(solution)/shard_map/others_0/ppermute | solution.py:43
  108.1 4.6 %collective-permute-start.29 = (bf16[224,1792]{1,0:T(8,128)(2,1)S(1)}, bf16[224,1792]{1,0:T(8,128)(2,1)S(1)}, u32[]{:S(2)}, u32[]{:S(2)}) collective-permute-start(bf16[224,1792]{1,0:T(8,128)(2,1)S(1)} %pad_maximum_fusion), channel_id=1, source_target_pairs={{0,1},{1,0},{2,3},{3,2},{4,5},{5,4},{6,7},{7,6},{8,9},{9,8},{10,11... | collective-permute-start | bytes 2408456 | tf_op jit(solution)/shard_map/others_1/ppermute | solution.py:43
  112.7 2.2 %finish.2.refs_7_ = f32[256,3584]{1,0:T(8,128)} custom-call(s32[5]{0:T(128)S(1)} %stack.23.place_ref, bf16[256,512]{1,0:T(8,128)(2,1)S(1)} %add_convert_fusion.g_ref, bf16[32,1792]{1,0:T(8,128)(2,1)S(1)} %add_convert_fusion.5.refs_0_, bf16[32,1792]{1,0:T(8,128)(2,1)S(1)} %collective-permute-done.36.refs_1_, ...), custom_call_target="tpu_custom_call" | custom-call | flops 469762048 | bytes 3670016 | tf_op jit(solution)/shard_map/finish/pallas_call | solution.py:114
  114.9 2.2 %finish.3 = f32[256,3584]{1,0:T(8,128)} custom-call(s32[5]{0:T(128)S(1)} %stack.23.place_ref, bf16[256,512]{1,0:T(8,128)(2,1)S(1)} %add_convert_fusion.g_ref, bf16[32,1792]{1,0:T(8,128)(2,1)S(1)} %add_convert_fusion.7.refs_0_, bf16[32,1792]{1,0:T(8,128)(2,1)S(1)} %collective-permute-done.24.refs_1_, ...), custom_call_target="tpu_custom_call", output_to_operand_aliasing={{}: (9, {})} | custom-call | flops 469762048 | bytes 3670016 | tf_op jit(solution)/shard_map/finish/pallas_call | solution.py:114
  (99 shorter events, 23.8 us)
Async XLA Ops:
  4.3 27.8 %collective-permute-start.13 = (bf16[3584,896]{1,0:T(8,128)(2,1)}, bf16[3584,896]{1,0:T(8,128)(2,1)}, u32[]{:S(2)}, u32[]{:S(2)}) collective-permute-start(bf16[3584,896]{1,0:T(8,128)(2,1)} %here_ref.1), channel_id=1, source_target_pairs={{0,1},{1,0},{2,3},{3,2},{4,5},{5,4},{6,7},{7,6},{8,9},{9,8},{10,11... | collective-permute-start | bytes 19267592 | tf_op jit(solution)/shard_map/basis_away/ppermute | solution.py:43
  5.7 5.5 %collective-permute-start.5 = (bf16[64,896]{1,0:T(8,128)(2,1)}, bf16[64,896]{1,0:T(8,128)(2,1)S(1)}, u32[]{:S(2)}, u32[]{:S(2)}) collective-permute-start(bf16[64,896]{1,0:T(8,128)(2,1)} %refs_0_.1), channel_id=1, source_target_pairs={{0,32},{32,0},{64,96},{96,64},{128,160},{160,128},{192,224},{224,1... | collective-permute-start | bytes 344072 | tf_op jit(solution)/shard_map/activations_1/ppermute | solution.py:257
  6.0 11.3 %collective-permute-start.8 = (bf16[64,896]{1,0:T(8,128)(2,1)}, bf16[64,896]{1,0:T(8,128)(2,1)S(1)}, u32[]{:S(2)}, u32[]{:S(2)}) collective-permute-start(bf16[64,896]{1,0:T(8,128)(2,1)} %refs_0_.1), channel_id=1, source_target_pairs={{0,128},{32,160},{64,192},{96,224},{128,0},{160,32},{192,64},{224,... | collective-permute-start | bytes 344072 | tf_op jit(solution)/shard_map/activations_4/ppermute | solution.py:257
  8.9 10.4 %collective-permute-start.10 = (bf16[64,896]{1,0:T(8,128)(2,1)}, bf16[64,896]{1,0:T(8,128)(2,1)S(1)}, u32[]{:S(2)}, u32[]{:S(2)}) collective-permute-start(bf16[64,896]{1,0:T(8,128)(2,1)} %refs_0_.1), channel_id=1, source_target_pairs={{0,192},{32,224},{64,0},{96,32},{128,64},{160,96},{192,128},{224,1... | collective-permute-start | bytes 344072 | tf_op jit(solution)/shard_map/activations_6/ppermute | solution.py:257
  9.7 9.6 %collective-permute-start.6 = (bf16[64,896]{1,0:T(8,128)(2,1)}, bf16[64,896]{1,0:T(8,128)(2,1)S(1)}, u32[]{:S(2)}, u32[]{:S(2)}) collective-permute-start(bf16[64,896]{1,0:T(8,128)(2,1)} %refs_0_.1), channel_id=1, source_target_pairs={{0,64},{32,96},{64,128},{96,160},{128,192},{160,224},{192,0},{224,... | collective-permute-start | bytes 344072 | tf_op jit(solution)/shard_map/activations_2/ppermute | solution.py:257
  11.2 15.4 %collective-permute-start.2 = (bf16[64,1024]{1,0:T(8,128)(2,1)S(1)}, bf16[64,1024]{1,0:T(8,128)(2,1)S(1)}, u32[]{:S(2)}, u32[]{:S(2)}) collective-permute-start(bf16[64,1024]{1,0:T(8,128)(2,1)S(1)} %pad_maximum_fusion.6.n0_ref), channel_id=1, source_target_pairs={{0,4},{1,13},{2,6},{3,15},{4,8},{5,1},{6,10},{7,3},{8,12},{9,5},{1... | collective-permute-start | bytes 393224 | tf_op jit(solution)/shard_map/n2/ppermute | solution.py:53
  19.3 5.6 %collective-permute-start.7 = (bf16[64,896]{1,0:T(8,128)(2,1)S(1)}, bf16[64,896]{1,0:T(8,128)(2,1)S(1)}, u32[]{:S(2)}, u32[]{:S(2)}) collective-permute-start(bf16[64,896]{1,0:T(8,128)(2,1)S(1)} %collective-permute-done.5.refs_1_), channel_id=1, source_target_pairs={{0,64},{32,96},{64,128},{96,160},{128,192},{160,224},{192,0},{224,... | collective-permute-start | bytes 344072 | tf_op jit(solution)/shard_map/activations_2/ppermute | solution.py:257
  19.3 5.6 %collective-permute-start.9 = (bf16[64,896]{1,0:T(8,128)(2,1)S(1)}, bf16[64,896]{1,0:T(8,128)(2,1)S(1)}, u32[]{:S(2)}, u32[]{:S(2)}) collective-permute-start(bf16[64,896]{1,0:T(8,128)(2,1)S(1)} %collective-permute-done.8.refs_4_), channel_id=1, source_target_pairs={{0,32},{32,0},{64,96},{96,64},{128,160},{160,128},{192,224},{224,1... | collective-permute-start | bytes 344072 | tf_op jit(solution)/shard_map/activations_1/ppermute | solution.py:257
  26.5 5.5 %collective-permute-start.12 = (bf16[256,896]{1,0:T(8,128)(2,1)S(1)}, bf16[256,896]{1,0:T(8,128)(2,1)S(1)}, u32[]{:S(2)}, u32[]{:S(2)}) collective-permute-start(bf16[256,896]{1,0:T(8,128)(2,1)S(1)} %get-tuple-element.20), channel_id=1, source_target_pairs={{0,1},{1,0},{2,3},{3,2},{4,5},{5,4},{6,7},{7,6},{8,9},{9,8},{10,11... | collective-permute-start | bytes 1376264 | tf_op jit(solution)/shard_map/x_away/ppermute | solution.py:43
  27.0 12.7 %collective-permute-start.3 = (bf16[128,1024]{1,0:T(8,128)(2,1)S(1)}, bf16[128,1024]{1,0:T(8,128)(2,1)S(1)}, u32[]{:S(2)}, u32[]{:S(2)}) collective-permute-start(bf16[128,1024]{1,0:T(8,128)(2,1)S(1)} %get-tuple-element.35), channel_id=1, source_target_pairs={{0,2},{1,15},{2,4},{3,1},{4,6},{5,3},{6,8},{7,5},{8,10},{9,7},{10,... | collective-permute-start | bytes 786440 | tf_op jit(solution)/shard_map/n13/ppermute | solution.py:48
  30.9 8.8 %collective-permute-start.4 = (bf16[32,1024]{1,0:T(8,128)(2,1)S(1)}, bf16[32,1024]{1,0:T(8,128)(2,1)S(1)}, u32[]{:S(2)}, u32[]{:S(2)}) collective-permute-start(bf16[32,1024]{1,0:T(8,128)(2,1)S(1)} %slice.90), channel_id=1, source_target_pairs={{0,4},{1,13},{2,6},{3,15},{4,8},{5,1},{6,10},{7,3},{8,12},{9,5},{1... | collective-permute-start | bytes 196616 | tf_op jit(solution)/shard_map/n4/ppermute | solution.py:53
  39.8 7.2 %collective-permute-start.14 = (bf16[224,1024]{1,0:T(8,128)(2,1)S(1)}, bf16[224,1024]{1,0:T(8,128)(2,1)S(1)}, u32[]{:S(2)}, u32[]{:S(2)}) collective-permute-start(bf16[224,1024]{1,0:T(8,128)(2,1)S(1)} %constant_dynamic-update-slice_fusion.7.near_ref), channel_id=1, source_target_pairs={{0,1},{1,0},{2,3},{3,2},{4,5},{5,4},{6,7},{7,6},{8,9},{9,8},{10,11... | collective-permute-start | bytes 1376264 | tf_op jit(solution)/shard_map/near_away/ppermute | solution.py:43
  42.7 5.3 %collective-permute-start.31 = (bf16[64,1792]{1,0:T(8,128)(2,1)S(1)}, bf16[64,1792]{1,0:T(8,128)(2,1)S(1)}, u32[]{:S(2)}, u32[]{:S(2)}) collective-permute-start(bf16[64,1792]{1,0:T(8,128)(2,1)S(1)} %pad_maximum_fusion.4), channel_id=1, source_target_pairs={{0,2},{1,15},{2,4},{3,1},{4,6},{5,3},{6,8},{7,5},{8,10},{9,7},{10,... | collective-permute-start | bytes 688136 | tf_op jit(solution)/shard_map/step2_0/ppermute | solution.py:48
  44.7 6.2 %collective-permute-start.19 = (bf16[64,1792]{1,0:T(8,128)(2,1)S(1)}, bf16[64,1792]{1,0:T(8,128)(2,1)S(1)}, u32[]{:S(2)}, u32[]{:S(2)}) collective-permute-start(bf16[64,1792]{1,0:T(8,128)(2,1)S(1)} %pad_maximum_fusion.2), channel_id=1, source_target_pairs={{0,2},{1,15},{2,4},{3,1},{4,6},{5,3},{6,8},{7,5},{8,10},{9,7},{10,... | collective-permute-start | bytes 688136 | tf_op jit(solution)/shard_map/step2_1/ppermute | solution.py:48
  48.1 5.8 %collective-permute-start.32 = (bf16[64,1792]{1,0:T(8,128)(2,1)S(1)}, bf16[64,1792]{1,0:T(8,128)(2,1)S(1)}, u32[]{:S(2)}, u32[]{:S(2)}) collective-permute-start(bf16[64,1792]{1,0:T(8,128)(2,1)S(1)} %add_convert_fusion.2), channel_id=1, source_target_pairs={{0,2},{1,15},{2,4},{3,1},{4,6},{5,3},{6,8},{7,5},{8,10},{9,7},{10,... | collective-permute-start | bytes 688136 | tf_op jit(solution)/shard_map/step3_0/ppermute | solution.py:48
  50.9 6.2 %collective-permute-start.20 = (bf16[64,1792]{1,0:T(8,128)(2,1)S(1)}, bf16[64,1792]{1,0:T(8,128)(2,1)S(1)}, u32[]{:S(2)}, u32[]{:S(2)}) collective-permute-start(bf16[64,1792]{1,0:T(8,128)(2,1)S(1)} %add_convert_fusion.4), channel_id=1, source_target_pairs={{0,2},{1,15},{2,4},{3,1},{4,6},{5,3},{6,8},{7,5},{8,10},{9,7},{10,... | collective-permute-start | bytes 688136 | tf_op jit(solution)/shard_map/step3_1/ppermute | solution.py:48
  53.4 13.5 %collective-permute-start.15 = (f32[256,512]{1,0:T(8,128)S(1)}, f32[256,512]{1,0:T(8,128)S(1)}, u32[]{:S(2)}, u32[]{:S(2)}) collective-permute-start(f32[256,512]{1,0:T(8,128)S(1)} %rotate_grads.1), channel_id=1, source_target_pairs={{0,64},{32,96},{64,0},{96,32},{128,192},{160,224},{192,128},{224,1... | collective-permute-start | bytes 1572872 | tf_op jit(solution)/shard_map/ppermute | solution.py:284
  53.9 6.2 %collective-permute-start.33 = (bf16[64,1792]{1,0:T(8,128)(2,1)S(1)}, bf16[64,1792]{1,0:T(8,128)(2,1)S(1)}, u32[]{:S(2)}, u32[]{:S(2)}) collective-permute-start(bf16[64,1792]{1,0:T(8,128)(2,1)S(1)} %add_convert_fusion.1), channel_id=1, source_target_pairs={{0,2},{1,15},{2,4},{3,1},{4,6},{5,3},{6,8},{7,5},{8,10},{9,7},{10,... | collective-permute-start | bytes 688136 | tf_op jit(solution)/shard_map/step4_0/ppermute | solution.py:48
  57.2 10.4 %collective-permute-start.21 = (bf16[64,1792]{1,0:T(8,128)(2,1)S(1)}, bf16[64,1792]{1,0:T(8,128)(2,1)S(1)}, u32[]{:S(2)}, u32[]{:S(2)}) collective-permute-start(bf16[64,1792]{1,0:T(8,128)(2,1)S(1)} %add_convert_fusion.3), channel_id=1, source_target_pairs={{0,2},{1,15},{2,4},{3,1},{4,6},{5,3},{6,8},{7,5},{8,10},{9,7},{10,... | collective-permute-start | bytes 688136 | tf_op jit(solution)/shard_map/step4_1/ppermute | solution.py:48
  60.1 9.8 %collective-permute-start.34 = (bf16[32,1792]{1,0:T(8,128)(2,1)S(1)}, bf16[32,1792]{1,0:T(8,128)(2,1)S(1)}, u32[]{:S(2)}, u32[]{:S(2)}) collective-permute-start(bf16[32,1792]{1,0:T(8,128)(2,1)S(1)} %slice.97), channel_id=1, source_target_pairs={{0,1},{1,0},{2,3},{3,2},{4,5},{5,4},{6,7},{7,6},{8,9},{9,8},{10,11... | collective-permute-start | bytes 344072 | tf_op jit(solution)/shard_map/other_0/ppermute | solution.py:43
  66.9 14.4 %collective-permute-start.16 = (f32[256,512]{1,0:T(8,128)S(1)}, f32[256,512]{1,0:T(8,128)S(1)}, u32[]{:S(2)}, u32[]{:S(2)}) collective-permute-start(f32[256,512]{1,0:T(8,128)S(1)} %add.61), channel_id=1, source_target_pairs={{0,128},{32,160},{64,192},{96,224},{128,0},{160,32},{192,64},{224,... | collective-permute-start | bytes 1572872 | tf_op jit(solution)/shard_map/ppermute | solution.py:291
  70.0 6.4 %collective-permute-start.35 = (bf16[32,1792]{1,0:T(8,128)(2,1)S(1)}, bf16[32,1792]{1,0:T(8,128)(2,1)S(1)}, u32[]{:S(2)}, u32[]{:S(2)}) collective-permute-start(bf16[32,1792]{1,0:T(8,128)(2,1)S(1)} %fusion.1), channel_id=1, source_target_pairs={{0,16},{1,17},{2,18},{3,19},{4,20},{5,21},{6,22},{7,23},{8,24},{9,... | collective-permute-start | bytes 344072 | tf_op jit(solution)/shard_map/across_0/ppermute | solution.py:58
  71.9 6.9 %collective-permute-start.23 = (bf16[32,1792]{1,0:T(8,128)(2,1)S(1)}, bf16[32,1792]{1,0:T(8,128)(2,1)S(1)}, u32[]{:S(2)}, u32[]{:S(2)}) collective-permute-start(bf16[32,1792]{1,0:T(8,128)(2,1)S(1)} %fusion), channel_id=1, source_target_pairs={{0,16},{1,17},{2,18},{3,19},{4,20},{5,21},{6,22},{7,23},{8,24},{9,... | collective-permute-start | bytes 344072 | tf_op jit(solution)/shard_map/across_1/ppermute | solution.py:58
  79.8 5.2 %collective-permute-start.37 = (bf16[64,1792]{1,0:T(8,128)(2,1)S(1)}, bf16[64,1792]{1,0:T(8,128)(2,1)S(1)}, u32[]{:S(2)}, u32[]{:S(2)}) collective-permute-start(bf16[64,1792]{1,0:T(8,128)(2,1)S(1)} %pad_maximum_fusion.5), channel_id=1, source_target_pairs={{0,2},{1,15},{2,4},{3,1},{4,6},{5,3},{6,8},{7,5},{8,10},{9,7},{10,... | collective-permute-start | bytes 688136 | tf_op jit(solution)/shard_map/a1_0/ppermute | solution.py:48
  81.3 14.0 %collective-permute-start.17 = (f32[256,512]{1,0:T(8,128)S(1)}, f32[256,512]{1,0:T(8,128)S(1)}, u32[]{:S(2)}, u32[]{:S(2)}) collective-permute-start(f32[256,512]{1,0:T(8,128)S(1)} %add.62), channel_id=1, source_target_pairs={{0,32},{32,0},{64,96},{96,64},{128,160},{160,128},{192,224},{224,1... | collective-permute-start | bytes 1572872 | tf_op jit(solution)/shard_map/ppermute | solution.py:299
  82.6 5.2 %collective-permute-start.25 = (bf16[64,1792]{1,0:T(8,128)(2,1)S(1)}, bf16[64,1792]{1,0:T(8,128)(2,1)S(1)}, u32[]{:S(2)}, u32[]{:S(2)}) collective-permute-start(bf16[64,1792]{1,0:T(8,128)(2,1)S(1)} %pad_maximum_fusion.3), channel_id=1, source_target_pairs={{0,2},{1,15},{2,4},{3,1},{4,6},{5,3},{6,8},{7,5},{8,10},{9,7},{10,... | collective-permute-start | bytes 688136 | tf_op jit(solution)/shard_map/a1_1/ppermute | solution.py:48
  85.0 5.3 %collective-permute-start.38 = (bf16[64,1792]{1,0:T(8,128)(2,1)S(1)}, bf16[64,1792]{1,0:T(8,128)(2,1)S(1)}, u32[]{:S(2)}, u32[]{:S(2)}) collective-permute-start(bf16[64,1792]{1,0:T(8,128)(2,1)S(1)} %collective-permute-done.37.refs_2_), channel_id=1, source_target_pairs={{0,2},{1,15},{2,4},{3,1},{4,6},{5,3},{6,8},{7,5},{8,10},{9,7},{10,... | collective-permute-start | bytes 688136 | tf_op jit(solution)/shard_map/a2_0/ppermute | solution.py:48
  93.0 5.4 %collective-permute-start.27 = (bf16[64,1792]{1,0:T(8,128)(2,1)S(1)}, bf16[64,1792]{1,0:T(8,128)(2,1)S(1)}, u32[]{:S(2)}, u32[]{:S(2)}) collective-permute-start(bf16[64,1792]{1,0:T(8,128)(2,1)S(1)} %collective-permute-done.26.refs_3_), channel_id=1, source_target_pairs={{0,2},{1,15},{2,4},{3,1},{4,6},{5,3},{6,8},{7,5},{8,10},{9,7},{10,... | collective-permute-start | bytes 688136 | tf_op jit(solution)/shard_map/a3_1/ppermute | solution.py:48
  95.5 5.5 %collective-permute-start.40 = (bf16[32,1792]{1,0:T(8,128)(2,1)S(1)}, bf16[32,1792]{1,0:T(8,128)(2,1)S(1)}, u32[]{:S(2)}, u32[]{:S(2)}) collective-permute-start(bf16[32,1792]{1,0:T(8,128)(2,1)S(1)} %slice.98), channel_id=1, source_target_pairs={{0,2},{1,15},{2,4},{3,1},{4,6},{5,3},{6,8},{7,5},{8,10},{9,7},{10,... | collective-permute-start | bytes 344072 | tf_op jit(solution)/shard_map/a4_0/ppermute | solution.py:48
  98.4 9.6 %collective-permute-start.28 = (bf16[32,1792]{1,0:T(8,128)(2,1)S(1)}, bf16[32,1792]{1,0:T(8,128)(2,1)S(1)}, u32[]{:S(2)}, u32[]{:S(2)}) collective-permute-start(bf16[32,1792]{1,0:T(8,128)(2,1)S(1)} %slice.93), channel_id=1, source_target_pairs={{0,2},{1,15},{2,4},{3,1},{4,6},{5,3},{6,8},{7,5},{8,10},{9,7},{10,... | collective-permute-start | bytes 344072 | tf_op jit(solution)/shard_map/a4_1/ppermute | solution.py:48
  101.1 11.6 %collective-permute-start.41 = (bf16[224,1792]{1,0:T(8,128)(2,1)S(1)}, bf16[224,1792]{1,0:T(8,128)(2,1)S(1)}, u32[]{:S(2)}, u32[]{:S(2)}) collective-permute-start(bf16[224,1792]{1,0:T(8,128)(2,1)S(1)} %pad_maximum_fusion.1), channel_id=1, source_target_pairs={{0,1},{1,0},{2,3},{3,2},{4,5},{5,4},{6,7},{7,6},{8,9},{9,8},{10,11... | collective-permute-start | bytes 2408456 | tf_op jit(solution)/shard_map/others_0/ppermute | solution.py:43
  108.1 6.8 %collective-permute-start.29 = (bf16[224,1792]{1,0:T(8,128)(2,1)S(1)}, bf16[224,1792]{1,0:T(8,128)(2,1)S(1)}, u32[]{:S(2)}, u32[]{:S(2)}) collective-permute-start(bf16[224,1792]{1,0:T(8,128)(2,1)S(1)} %pad_maximum_fusion), channel_id=1, source_target_pairs={{0,1},{1,0},{2,3},{3,2},{4,5},{5,4},{6,7},{7,6},{8,9},{9,8},{10,11... | collective-permute-start | bytes 2408456 | tf_op jit(solution)/shard_map/others_1/ppermute | solution.py:43
  (12 other events, 49.9 us)
